TPU v7x, 32 devices: a whole 2x2x4 slice. The times are simulated.
32 devices in a mesh: groups: 2 (over x), cells: 16 (over z, y, core).
Axes of the slice: x: 2, y: 2, z: 4, core: 2. Of those that a mesh axis runs over, the one named last changes fastest.
Arguments:
- points: float32 [3, 2097152], P(None, ('groups', 'cells')), parts along dimension 1, may hold values from -6 to 2049, as said below
- centroids: float32 [3, 524288], P(None, ('groups', 'cells')), parts along dimension 1, may hold values from -6 to 2049, as said below
- pair_blocks: int32 [16384, 6], P(('groups', 'cells')), parts along dimension 0, may hold values from 0 to 2047, as said below
- pair_count: int32 [16384], P(('groups', 'cells')), parts along dimension 0, may hold values from 1 to 6, as said below
- centroid_nbrs: int32 [4096, 3], P(('groups', 'cells')), parts along dimension 0, may hold values from 0 to 2047, as said below
- sigma2: float32 [2], P('groups'), parts along dimension 0, may hold values from 2 to 4
Outputs:
- displacement: float32 [3, 524288], P(None, ('groups', 'cells')), parts along dimension 1
- sigma2_new: float32 [2], P('groups'), parts along dimension 0
There are 2 independent parts, one for each index of `groups`. A program takes and returns all parts, laid end to end along the dimension named above; each array names one. Nothing has to cross between parts.
Inputs may be any that keep to these rules, and one draw needn't show every extreme that they name: `points`: point coordinates: along track between the point block's home block b // 4 and the next, across track in [0, 1), heights of either sign. `centroids`: centroid coordinates: along track between the block's index and the next, across track in [0, 1), heights of either sign. `pair_blocks`: A row lists 6 distinct blocks out of the 7 consecutive blocks starting at min(max(h - 3, 0), 2041), h = b // 4 the home block of point block b. Only the first pair_count entries of a row of pair_blocks are used. `centroid_nbrs`: A row starts with the block itself, then lists distinct other blocks out of the 7 consecutive blocks starting at min(max(c - 3, 0), 2041), c the row's block.
All inputs are finite; a program needn't handle non-finite values.
Results may differ from a plain program's by a relative error of at most 0.0003.
Values sent between devices are 32-bit elements; how exact they have to be, the bound alone decides.
A program may use at most 128 MiB of HBM per device.

v0:
```python
import math

import jax
import jax.numpy as jnp
from jax import lax
from jax.sharding import PartitionSpec as P

REACH = 3
SMOOTH = 4


OUTLIER = 0.2
SHRINK = 1.0
KERNEL_VAR = 0.5


def padded(x, sides, width):
    for axis, dim in sides:
        size, length = (lax.axis_size(axis), x.shape[dim])
        up = [(i, (i + 1) % size) for i in range(size - 1)]
        down = [(j, i) for i, j in up]
        last = lax.slice_in_dim(x, length - width, length, axis=dim)
        first = lax.slice_in_dim(x, 0, width, axis=dim)
        before = lax.ppermute(last, axis, up)
        after = lax.ppermute(first, axis, down)
        x = jnp.concatenate([before, x, after], axis=dim)
    return x


def from_behind(block, axis, distance):
    devices = range(lax.axis_size(axis))
    route = [(i - distance, i) for i in devices if i - distance in devices]
    return lax.ppermute(block, axis, route)


def body(points, centroids, pair_blocks, pair_count, centroid_nbrs, sigma2):
    index_here = lax.axis_index("cells")
    pts_dev = points.shape[1]
    cen_dev = centroids.shape[1]
    nblk = cen_dev // 128
    pblk = pts_dev // 128
    half_blocks = pblk // 2
    pts_three = points.reshape(3, pblk, 128)
    extended = padded(centroids, (("cells", 1),), cen_dev)
    wblk = cen_dev // 128
    nbuf = nblk + 2 * wblk
    ext_blocks = extended.reshape(3, nbuf, 128)
    first_block = index_here * nblk - wblk
    var_old = sigma2[0]
    outlier = (2.0 * math.pi * var_old) ** 1.5 * (OUTLIER / (1.0 - OUTLIER)) * (cen_dev / pts_dev)
    group_size = min(64, half_blocks)
    ngroup = pblk // group_size
    window_blocks = group_size // 4 + 2 * REACH
    local_lists = pair_blocks - first_block
    window_ids = jnp.arange(window_blocks, dtype=jnp.int32)

    def group_step(state_in, gidx):
        sums_buf, spread, count = state_in
        point_tile = lax.dynamic_slice_in_dim(pts_three, gidx * group_size, group_size, 1)
        slot_lists = lax.dynamic_slice_in_dim(local_lists, gidx * group_size, group_size, 0)
        counts = lax.dynamic_slice_in_dim(pair_count, gidx * group_size, group_size, 0)
        slot_limit = jnp.max(counts)
        window_base = jnp.clip(jnp.min(slot_lists), 0, nbuf - window_blocks)

        def slot_tile(slot):
            slot_local = lax.dynamic_index_in_dim(slot_lists, slot, 1, keepdims=False)
            cen_tile = jnp.take(ext_blocks, slot_local, axis=1)
            differences = [
                point_tile[component][:, None, :] - cen_tile[component][:, :, None]
                for component in range(3)
            ]
            distance2 = (
                differences[0] * differences[0]
                + differences[1] * differences[1]
                + differences[2] * differences[2]
            )
            alive_mask = (slot < counts).astype(jnp.float32)
            affinity = jnp.exp(-distance2 / (2.0 * var_old)) * alive_mask[:, None, None]
            return (slot_local, differences, distance2, affinity)

        def first_pass(slot, weight_sum):
            return weight_sum + jnp.sum(slot_tile(slot)[3], axis=1)

        weight_sum = lax.fori_loop(
            0, slot_limit, first_pass, jnp.zeros((group_size, 128), jnp.float32)
        )
        normaliser = weight_sum + outlier

        def second_pass(slot, running):
            acc_window, acc_spread = running
            slot_local, differences, distance2, affinity = slot_tile(slot)
            resp = affinity / normaliser[:, None, :]
            block_terms = jnp.stack(
                [jnp.sum(resp, axis=2)]
                + [jnp.sum(resp * part_diff, axis=2) for part_diff in differences],
                axis=0,
            )
            onehot = ((slot_local - window_base)[:, None] == window_ids[None, :]).astype(
                jnp.float32
            )
            acc_window = acc_window + jnp.einsum(
                "gb,kgm->kbm", onehot, block_terms, precision=lax.Precision.HIGHEST
            )
            return (acc_window, acc_spread + jnp.sum(resp * distance2))

        acc_window, spread = lax.fori_loop(
            0, slot_limit, second_pass, (jnp.zeros((4, window_blocks, 128), jnp.float32), spread)
        )
        current = lax.dynamic_slice_in_dim(sums_buf, window_base, window_blocks, 1)
        sums_buf = lax.dynamic_update_slice_in_dim(sums_buf, current + acc_window, window_base, 1)
        count = count + jnp.sum(weight_sum / normaliser)
        return ((sums_buf, spread, count), None)

    init = (
        jnp.zeros((4, nbuf, 128), jnp.float32),
        jnp.zeros((), jnp.float32),
        jnp.zeros((), jnp.float32),
    )
    (sums_buf, spread, count), _ = lax.scan(group_step, init, jnp.arange(ngroup))
    left_rim = sums_buf[:, :wblk]
    owned = sums_buf[:, wblk : wblk + nblk]
    right_rim = sums_buf[:, wblk + nblk :]
    from_right = from_behind(left_rim, "cells", -1)
    from_left = from_behind(right_rim, "cells", 1)
    owned = owned + from_left
    owned = owned + from_right
    mass = owned[0]
    pull = owned[1:4]
    motion = pull / (mass[None] + SHRINK)
    reach_cols = REACH * 128
    offset_cols = cen_dev - reach_cols
    pos_ext = lax.slice_in_dim(
        extended, offset_cols, offset_cols + cen_dev + 2 * reach_cols, axis=1
    ).reshape(3, nblk + 2 * REACH, 128)
    own_pos = centroids.reshape(3, nblk, 128)
    nbr_lists = centroid_nbrs - (index_here * nblk - REACH)
    sgroup = min(16, nblk)
    nsgroup = nblk // sgroup

    def group_kernel(gidx):
        own_tile = lax.dynamic_slice_in_dim(own_pos, gidx * sgroup, sgroup, 1)
        nbr_local = lax.dynamic_slice_in_dim(nbr_lists, gidx * sgroup, sgroup, 0)
        nbr_tile = jnp.take(pos_ext, nbr_local, axis=1)
        pieces = [
            own_tile[component][:, None, :, None] - nbr_tile[component][:, :, None, :]
            for component in range(3)
        ]
        distance2 = pieces[0] * pieces[0] + pieces[1] * pieces[1] + pieces[2] * pieces[2]
        kernel = jnp.exp(-distance2 / (2.0 * KERNEL_VAR))
        return (kernel, jnp.sum(kernel, axis=(1, 3)))

    kernels, kernel_sums = lax.map(group_kernel, jnp.arange(nsgroup))
    for step in range(SMOOTH):
        motion_ext = padded(motion.reshape(3, cen_dev), (("cells", 1),), reach_cols)
        motion_ext = motion_ext.reshape(3, nblk + 2 * REACH, 128)

        def group_smooth(inputs):
            gidx, kernel, kernel_sum = inputs
            nbr_local = lax.dynamic_slice_in_dim(nbr_lists, gidx * sgroup, sgroup, 0)
            nbr_motion = jnp.take(motion_ext, nbr_local, axis=1)
            weighted = jnp.einsum(
                "sjab,ksjb->ksa", kernel, nbr_motion, precision=lax.Precision.HIGHEST
            )
            return weighted / kernel_sum[None]

        smoothed = lax.map(group_smooth, (jnp.arange(nsgroup), kernels, kernel_sums))
        motion = smoothed.transpose(1, 0, 2, 3).reshape(3, nblk, 128)
    cross_loc = jnp.sum(pull * motion)
    energy_loc = jnp.sum(mass[None] * motion * motion)
    spread_all, count_all, cross_all, energy_all = lax.psum(
        (spread, count, cross_loc, energy_loc), "cells"
    )
    sigma_new = (spread_all - 2.0 * cross_all + energy_all) / (3.0 * count_all)
    return (motion.reshape(3, cen_dev), jnp.reshape(sigma_new, (1,)))


def solution(mesh):
    return jax.shard_map(
        body,
        mesh=mesh,
        in_specs=(
            P(None, ("groups", "cells")),
            P(None, ("groups", "cells")),
            P(("groups", "cells"), None),
            P(("groups", "cells")),
            P(("groups", "cells"), None),
            P("groups"),
        ),
        out_specs=(P(None, ("groups", "cells")), P("groups")),
        check_vma=False,
    )
```

profile of v0, /device:TPU:0, one launch (start us, length us, event | category | flops | bytes accessed | tf_op | source)
XLA Modules:
  0.0 1282.0 jit_solution(15249787858450718619)
XLA Ops:
  9.0 338.1 %while.113 = (s32[]{:T(128)}, f32[4,384,128]{2,1,0:T(8,128)S(1)}, f32[]{:T(128)}, f32[]{:T(128)}, s32[8]{0:T(128)S(1)}, /*index=5*/s32[512,6]{0,1:T(8,128)S(1)},...) while((s32[]{:T(128)}, f32[4,384,128]{2,1,0:T(8,128)S(1)}, ...), condition=%wide.region_17.20_spmd.clone, body=%wide.region_3.19_spmd.clone.sunk | while | flops 43420556 | bytes 3064917 | solution.py:119
  12.6 12.1 while.114
  26.0 24.4 %while.115 = (s32[]{:T(128)}, f32[4,22,128]{2,1,0:T(8,128)S(1)}, f32[]{:T(128)}, s32[]{:T(128)}, f32[3,64,128]{2,1,0:T(8,128)S(1)}, /*index=5*/s32[64,6]{0,1:T(8...) while((s32[]{:T(128)}, f32[4,22,128]{2,1,0:T(8,128)S(1)}, ...), condition=%wide.region_15.17_spmd, body=%wide.region_9.16_spmd.sunk | while | flops 30775236 | bytes 1375147 | solution.py:106
  27.7 9.4 fusion.161
  39.5 9.4 fusion.161
  54.9 12.1 while.114
  68.3 24.4 %while.115 = (s32[]{:T(128)}, f32[4,22,128]{2,1,0:T(8,128)S(1)}, f32[]{:T(128)}, s32[]{:T(128)}, f32[3,64,128]{2,1,0:T(8,128)S(1)}, /*index=5*/s32[64,6]{0,1:T(8...) while((s32[]{:T(128)}, f32[4,22,128]{2,1,0:T(8,128)S(1)}, ...), condition=%wide.region_15.17_spmd, body=%wide.region_9.16_spmd.sunk | while | flops 30775236 | bytes 1375147 | solution.py:106
  69.9 9.4 fusion.161
  81.8 9.4 fusion.161
  97.1 12.1 while.114
  110.6 24.4 %while.115 = (s32[]{:T(128)}, f32[4,22,128]{2,1,0:T(8,128)S(1)}, f32[]{:T(128)}, s32[]{:T(128)}, f32[3,64,128]{2,1,0:T(8,128)S(1)}, /*index=5*/s32[64,6]{0,1:T(8...) while((s32[]{:T(128)}, f32[4,22,128]{2,1,0:T(8,128)S(1)}, ...), condition=%wide.region_15.17_spmd, body=%wide.region_9.16_spmd.sunk | while | flops 30775236 | bytes 1375147 | solution.py:106
  112.2 9.4 fusion.161
  124.1 9.4 fusion.161
  139.4 12.1 while.114
  152.8 24.4 %while.115 = (s32[]{:T(128)}, f32[4,22,128]{2,1,0:T(8,128)S(1)}, f32[]{:T(128)}, s32[]{:T(128)}, f32[3,64,128]{2,1,0:T(8,128)S(1)}, /*index=5*/s32[64,6]{0,1:T(8...) while((s32[]{:T(128)}, f32[4,22,128]{2,1,0:T(8,128)S(1)}, ...), condition=%wide.region_15.17_spmd, body=%wide.region_9.16_spmd.sunk | while | flops 30775236 | bytes 1375147 | solution.py:106
  154.5 9.4 fusion.161
  166.3 9.4 fusion.161
  181.7 12.1 while.114
  195.1 24.4 %while.115 = (s32[]{:T(128)}, f32[4,22,128]{2,1,0:T(8,128)S(1)}, f32[]{:T(128)}, s32[]{:T(128)}, f32[3,64,128]{2,1,0:T(8,128)S(1)}, /*index=5*/s32[64,6]{0,1:T(8...) while((s32[]{:T(128)}, f32[4,22,128]{2,1,0:T(8,128)S(1)}, ...), condition=%wide.region_15.17_spmd, body=%wide.region_9.16_spmd.sunk | while | flops 30775236 | bytes 1375147 | solution.py:106
  196.7 9.4 fusion.161
  208.6 9.4 fusion.161
  223.9 12.1 while.114
  237.4 24.4 %while.115 = (s32[]{:T(128)}, f32[4,22,128]{2,1,0:T(8,128)S(1)}, f32[]{:T(128)}, s32[]{:T(128)}, f32[3,64,128]{2,1,0:T(8,128)S(1)}, /*index=5*/s32[64,6]{0,1:T(8...) while((s32[]{:T(128)}, f32[4,22,128]{2,1,0:T(8,128)S(1)}, ...), condition=%wide.region_15.17_spmd, body=%wide.region_9.16_spmd.sunk | while | flops 30775236 | bytes 1375147 | solution.py:106
  239.0 9.4 fusion.161
  250.8 9.4 fusion.161
  266.2 12.1 while.114
  279.6 24.4 %while.115 = (s32[]{:T(128)}, f32[4,22,128]{2,1,0:T(8,128)S(1)}, f32[]{:T(128)}, s32[]{:T(128)}, f32[3,64,128]{2,1,0:T(8,128)S(1)}, /*index=5*/s32[64,6]{0,1:T(8...) while((s32[]{:T(128)}, f32[4,22,128]{2,1,0:T(8,128)S(1)}, ...), condition=%wide.region_15.17_spmd, body=%wide.region_9.16_spmd.sunk | while | flops 30775236 | bytes 1375147 | solution.py:106
  281.3 9.4 fusion.161
  293.1 9.4 fusion.161
  308.5 12.1 while.114
  321.9 24.4 %while.115 = (s32[]{:T(128)}, f32[4,22,128]{2,1,0:T(8,128)S(1)}, f32[]{:T(128)}, s32[]{:T(128)}, f32[3,64,128]{2,1,0:T(8,128)S(1)}, /*index=5*/s32[64,6]{0,1:T(8...) while((s32[]{:T(128)}, f32[4,22,128]{2,1,0:T(8,128)S(1)}, ...), condition=%wide.region_15.17_spmd, body=%wide.region_9.16_spmd.sunk | while | flops 30775236 | bytes 1375147 | solution.py:106
  323.5 9.4 fusion.161
  335.4 9.4 fusion.161
  347.9 6.6 collective-permute-start.2
  355.9 563.4 %collective-permute-done.3 = f32[4,128,128]{2,1,0:T(8,128)} collective-permute-done((f32[4,128,128]{2,1,0:T(8,128)S(1)}, f32[4,128,128]{2,1,0:T(8,128)}, u32[]{:S(2)}, u32[]{:S(2)}) %collective-permute-start.3) | collective-permute-done | bytes 262176 | tf_op jit(solution)/shard_map/ppermute | solution.py:33
  920.5 7.1 collective-permute-start.4
  928.9 50.2 %while.106 = (s32[]{:T(128)}, f32[8,16,3,128,128]{4,3,2,1,0:T(8,128)}, f32[8,16,128]{2,1,0:T(8,128)S(1)}, s32[8]{0:T(128)S(1)}, f32[3,128,128]{2,1,0:T(8,128)S(1...) while((s32[]{:T(128)}, ...), condition=%wide.region_2.4_spmd, body=%wide.region_0.3_spmd.sunk | while | flops 14959912 | bytes 3864515 | solution.py:152
  979.2 59.8 %while.107 = (s32[]{:T(128)}, f32[8,3,16,128]{3,1,2,0:T(4,128)S(1)}, s32[8]{0:T(128)S(1)}, s32[128,3]{1,0:T(8,128)S(1)}, f32[3,134,128]{2,0,1:T(4,128)S(1)}, /*i...) while((s32[]{:T(128)}, f32[8,3,16,128]{3,1,2,0:T(4,128)S(1)}, ...), condition=%wide.region_19.22_spmd, body=%wide.region_18.21_spmd.sunk | while | flops 28337444 | bytes 3602831 | solution.py:166
  981.4 5.4 fusion.142
  988.8 5.4 fusion.142
  996.3 5.4 fusion.142
  1003.8 5.4 fusion.142
  1011.3 5.4 fusion.142
  1018.8 5.4 fusion.142
  1026.2 5.4 fusion.142
  1033.7 5.4 fusion.142
  1046.9 59.8 %while.108 = (s32[]{:T(128)}, f32[8,3,16,128]{3,1,2,0:T(4,128)S(1)}, s32[8]{0:T(128)S(1)}, s32[128,3]{1,0:T(8,128)S(1)}, f32[3,134,128]{2,0,1:T(4,128)S(1)}, /*i...) while((s32[]{:T(128)}, f32[8,3,16,128]{3,1,2,0:T(4,128)S(1)}, ...), condition=%wide.region_21.24_spmd, body=%wide.region_20.23_spmd.sunk | while | flops 28337444 | bytes 3602831 | solution.py:166
  1049.1 5.4 fusion.146
  1056.5 5.4 fusion.146
  1064.0 5.4 fusion.146
  1071.5 5.4 fusion.146
  1079.0 5.4 fusion.146
  1086.4 5.4 fusion.146
  1093.9 5.4 fusion.146
  1101.4 5.4 fusion.146
  1114.2 59.8 %while.109 = (s32[]{:T(128)}, f32[8,3,16,128]{3,1,2,0:T(4,128)S(1)}, s32[8]{0:T(128)S(1)}, s32[128,3]{1,0:T(8,128)S(1)}, f32[3,134,128]{2,0,1:T(4,128)S(1)}, /*i...) while((s32[]{:T(128)}, f32[8,3,16,128]{3,1,2,0:T(4,128)S(1)}, ...), condition=%wide.region_23.26_spmd, body=%wide.region_22.25_spmd.sunk | while | flops 28337444 | bytes 3602831 | solution.py:166
  1116.4 5.4 fusion.150
  1123.8 5.4 fusion.150
  1131.3 5.4 fusion.150
  1161.2 5.4 fusion.150
  1174.0 5.6 collective-permute-start.10
  1182.9 59.8 %while.110 = (s32[]{:T(128)}, f32[8,3,16,128]{3,1,2,0:T(4,128)S(1)}, s32[8]{0:T(128)S(1)}, s32[128,3]{1,0:T(8,128)S(1)}, f32[3,134,128]{2,0,1:T(4,128)S(1)}, /*i...) while((s32[]{:T(128)}, f32[8,3,16,128]{3,1,2,0:T(4,128)S(1)}, ...), condition=%wide.region_25.28_spmd, body=%wide.region_24.27_spmd.sunk | while | flops 28337444 | bytes 3602831 | solution.py:166
  1222.4 5.4 fusion.154
  1244.1 34.2 %all-reduce = (f32[]{:T(128)}, f32[]{:T(128)}, f32[]{:T(128)}, f32[]{:T(128)}) all-reduce(f32[]{:T(128)} %get-tuple-element.599, f32[]{:T(128)} %fusion.102, f32[]{:T(128)} %fusion.101, f32[]{:T(128)} %get-tuple-element.600), channel_id=1, replica_groups=mesh['groups'=2,'cells'=16] {'cells'}, use_global_device_ids=true, to_apply=%region_26.29 | all-reduce | flops 4 | bytes 32 | tf_op jit(solution)/shard_map/psum | solution.py:170
  (721 shorter events, 308.4 us)
Async XLA Ops:
  0.6 7.2 collective-permute-start
  3.0 5.9 collective-permute-start.1
  9.0 346.8 %copy-start.1 = (f32[3,16384]{1,0:T(4,128)S(1)}, f32[3,16384]{1,0:T(4,128)}, u32[]{:S(2)}) copy-start(f32[3,16384]{1,0:T(4,128)} %param.27) | copy-start | bytes 589828
  347.9 8.0 collective-permute-start.2
  354.5 564.8 %collective-permute-start.3 = (f32[4,128,128]{2,1,0:T(8,128)S(1)}, f32[4,128,128]{2,1,0:T(8,128)}, u32[]{:S(2)}, u32[]{:S(2)}) collective-permute-start(f32[4,128,128]{2,1,0:T(8,128)S(1)} %get-tuple-element.810), channel_id=1, source_target_pairs={{1,0},{2,1},{3,2},{4,3},{5,4},{6,5},{7,6},{8,7},{9,8},{10,9},{11,1... | collective-permute-start | bytes 786440 | tf_op jit(solution)/shard_map/ppermute | solution.py:33
  920.5 58.7 %collective-permute-start.4 = (f32[3,384]{1,0:T(4,128)S(1)}, f32[3,384]{1,0:T(4,128)S(1)}, u32[]{:S(2)}, u32[]{:S(2)}) collective-permute-start(f32[3,384]{1,0:T(4,128)S(1)} %get-tuple-element.819), channel_id=1, source_target_pairs={{0,1},{1,2},{2,3},{3,4},{4,5},{5,6},{6,7},{7,8},{8,9},{9,10},{10,1... | collective-permute-start | bytes 13832 | tf_op jit(solution)/shard_map/ppermute | solution.py:24
  927.5 51.6 %collective-permute-start.5 = (f32[3,384]{1,0:T(4,128)S(1)}, f32[3,384]{1,0:T(4,128)S(1)}, u32[]{:S(2)}, u32[]{:S(2)}) collective-permute-start(f32[3,384]{1,0:T(4,128)S(1)} %get-tuple-element.820), channel_id=1, source_target_pairs={{1,0},{2,1},{3,2},{4,3},{5,4},{6,5},{7,6},{8,7},{9,8},{10,9},{11,1... | collective-permute-start | bytes 13832 | tf_op jit(solution)/shard_map/ppermute | solution.py:25
  1039.1 4.5 collective-permute-start.6
  1042.1 4.7 collective-permute-start.7
  1106.8 5.6 collective-permute-start.8
  1111.0 3.1 collective-permute-start.9
  1174.0 6.9 collective-permute-start.10
  1179.7 3.1 collective-permute-start.11
  1242.7 38.2 %copy-start = (f32[8,3,16,128]{3,1,2,0:T(4,128)}, f32[8,3,16,128]{3,1,2,0:T(4,128)S(1)}, u32[]{:S(2)}) copy-start(f32[8,3,16,128]{3,1,2,0:T(4,128)S(1)} %get-tuple-element.598) | copy-start | bytes 589828
where the time goes:
time: 1290 us; the launch traced here: 1280 us
  waiting for transfers between devices  570 us (44%)
  other arithmetic  283 us (22%)
  matrix products  175 us (14%)
  loops' own time  89.2 us (7%)
  local copies, waits for them, and re-layouts  88.1 us (7%)
  starting transfers between devices  36.9 us (3%)
  blocking collectives  34.2 us (3%)
    ppermute x2, waiting for transfers between devices, from_behind(): return lax.ppermute(block, axis, route)  563 us
    dot_general x32, matrix products, group_smooth(): jnp.einsum('sjab,ksjb->ksa', kernel, nbr_motion, precision=lax.Precision....  171 us
    reduce_sum x16, other arithmetic, second_pass(): return (acc_window, acc_spread + jnp.sum(resp * distance2))  150 us
    reduce_sum x16, other arithmetic, first_pass(): return weight_sum + jnp.sum(slot_tile(slot)[3], axis=1)  64.8 us
    psum x1, blocking collectives, body(): lax.psum((spread, count, cross_loc, energy_loc), 'cells')  34.2 us
    dynamic_slice x48, local copies, waits for them, and re-layouts, body(): lax.scan(group_step, init, jnp.arange(ngroup))  28.9 us
    another operation x8, loops' own time, group_step(): lax.fori_loop(0, slot_limit, second_pass, (jnp.zeros((4, window_blocks, 1...  27.5 us
  transfers between devices with their start and end apart: 12, of which 4 were waited for; matrix products, arithmetic and copies ran while one was open for 4% of the time, Pallas kernels for 0%

commit v1 on v0

v1 whole, which is shorter than its diff:
```python
import functools
import math

import jax
import jax.numpy as jnp
from jax import lax
from jax.experimental import pallas as pl
from jax.experimental.pallas import tpu as pltpu
from jax.sharding import PartitionSpec as P

REACH = 3
SMOOTH = 4
OUTLIER = 0.2
SHRINK = 1.0
KERNEL_VAR = 0.5
LOG2E = 1.4426950408889634

F32, BF16 = jnp.float32, jnp.bfloat16
KF = 32
H = 16
WIN = 24
DUMMY = WIN - 1
UNROLL = 4
HALO = 24
FRONT = 16


def split3(v):
    high = v.astype(BF16).astype(F32)
    rest = v - high
    mid = rest.astype(BF16).astype(F32)
    return high, mid, rest - mid


def lane_features(ref_a, ref_z, x, y, z, scale, root):
    rows = x.shape[0]
    ones = jnp.ones_like(x)
    x1, x2, x3 = split3(x)
    y1, y2, y3 = split3(y)
    own = split3(-scale * (x * x + y * y))
    height = split3(-root * z)
    half_a = [x1, x2, x1, x2, x3, x1, y1, y2, y1, y2, y3, y1, ones, ones, ones, *own]
    for k, v in enumerate(half_a):
        ref_a[pl.ds(k, rows, stride=KF), :] = v
    for k, v in enumerate([*height, ones, ones, ones]):
        ref_z[pl.ds(15 + k, rows, stride=KF), :] = v


def row_features(ref_t, x, y, z, scale, root, dead=None):
    rows = x.shape[0]
    ones = jnp.ones_like(x)
    x1, x2, x3 = split3(2.0 * scale * x)
    y1, y2, y3 = split3(2.0 * scale * y)
    own = -scale * (x * x + y * y)
    if dead is not None:
        own = jnp.where(dead, -1e9, own)
    feats = [x1, x1, x2, x2, x1, x3, y1, y1, y2, y2, y1, y3, *split3(own), ones, ones, ones]
    for k, v in enumerate(feats + list(split3(root * z))):
        ref_t[pl.ds(k, rows, stride=KF), :] = v


def transpose_features(ref_t, table):
    def step(i, carry):
        for u in range(4):
            j = i * 4 + u
            block = ref_t[pl.ds(pl.multiple_of(j * KF, KF), KF), :]
            table[j] = block.T.astype(BF16)
        return carry

    lax.fori_loop(0, WIN // 4, step, 0)


def pair_weights(table, ref_a, ref_z, l, b):
    at = pl.ds(pl.multiple_of(b * KF, KF), KF)
    right = jnp.concatenate([ref_a[at, :].astype(BF16), ref_z[at, :].astype(BF16)], axis=1)
    d = jnp.dot(table[l], right, preferred_element_type=F32)
    dz = d[:, 128:]
    return jnp.exp2(d[:, :128] - dz * dz)


def pair_kernel(
    nslot, per_home, nchunk, lists, counts, totals, first, sigma2, pts, cen,
    sums, stats, ref_a, ref_z, ref_t, table, wbuf, wacc, rbuf, acc, bsel, lsel,
):
    ch = H * per_home
    var = sigma2[0]
    scale_v = LOG2E / (2.0 * jnp.full((1, 128), var, F32))
    root_v = jnp.sqrt(scale_v)
    base_v = 2.0 * math.pi * jnp.full((1, 128), var, F32)
    outlier = base_v * jnp.sqrt(base_v) * (OUTLIER / (1.0 - OUTLIER) / per_home)
    for ref in (ref_a, ref_z, ref_t, rbuf):
        ref[...] = jnp.zeros_like(ref)
    sums[...] = jnp.zeros_like(sums)

    def chunk(ck, carry):
        spread, count = carry
        prow = pl.ds(pl.multiple_of(ck * ch, ch), ch)
        crow = pl.ds(pl.multiple_of(ck * H, H), WIN)
        origin = (first[0] + ck * H + H // 2).astype(F32)
        px, py = pts[0, prow, :] - origin, pts[1, prow, :]
        cx, cy = cen[0, crow, :] - origin, cen[1, crow, :]
        z0 = pts[2, pl.ds(pl.multiple_of(ck * ch, ch), 8), :][0:1, 0:1]
        pz = pts[2, prow, :] - z0
        cz = cen[2, crow, :] - z0
        lane_features(ref_a, ref_z, px, py, pz, scale_v, root_v)
        dead = lax.broadcasted_iota(jnp.int32, (WIN, 128), 0) == DUMMY
        row_features(ref_t, cx, cy, cz, scale_v, root_v, dead)
        transpose_features(ref_t, table)
        wacc[...] = jnp.zeros_like(wacc)
        acc[...] = jnp.zeros_like(acc)
        total = totals[ck]
        steps = (total + UNROLL - 1) // UNROLL

        def first_pass(i, state):
            b, s = state
            for u in range(UNROLL):
                k = i * UNROLL + u
                bb = jnp.minimum(b, ch - 1)
                at = ck * ch + bb
                l = lists[at * nslot + s] - ck * H
                l = jnp.where(k < total, l, DUMMY)
                bsel[k] = bb
                lsel[k] = l
                w = pair_weights(table, ref_a, ref_z, l, bb)
                wbuf[k] = w.astype(BF16)
                wrow = pl.ds(pl.multiple_of(bb * 8, 8), 8)
                wacc[wrow, :] += jnp.sum(w.reshape(16, 8, 128), axis=0)
                more = s + 1 < counts[at]
                b = jnp.where(more, b, b + 1)
                s = jnp.where(more, s + 1, 0)
            return b, s

        lax.fori_loop(0, steps, first_pass, (jnp.int32(0), jnp.int32(0)))
        weight = wacc[pl.ds(0, ch, stride=8), :]
        for i in range(1, 8):
            weight = weight + wacc[pl.ds(i, ch, stride=8), :]
        inv = 1.0 / (weight + outlier)
        count = count + weight * inv
        square = px * px + py * py + pz * pz
        feats = [inv, inv * px, inv * py, inv * pz, inv * square]
        for k, v in enumerate(feats):
            for t, piece in enumerate(split3(v)):
                rbuf[pl.ds(3 * k + t, ch, stride=16), :] = piece

        def second_pass(i, carry):
            for u in range(UNROLL):
                k = i * UNROLL + u
                b, l = bsel[k], lsel[k]
                r = rbuf[pl.ds(pl.multiple_of(b * 16, 16), 16), :].astype(BF16)
                o = lax.dot_general(
                    r, wbuf[k], (((1,), (1,)), ((), ())), preferred_element_type=F32
                )
                arow = pl.ds(pl.multiple_of(l * 16, 16), 16)
                acc[arow, :] += o
            return carry

        lax.fori_loop(0, steps, second_pass, 0)
        got = []
        for k in range(5):
            v = acc[pl.ds(3 * k, WIN, stride=16), :]
            v = v + acc[pl.ds(3 * k + 1, WIN, stride=16), :]
            got.append(v + acc[pl.ds(3 * k + 2, WIN, stride=16), :])
        mass, sx, sy, sz, sq = got
        pull_x, pull_y, pull_z = sx - cx * mass, sy - cy * mass, sz - cz * mass
        term = sq - (cx * sx + cy * sy + cz * sz) - (cx * pull_x + cy * pull_y + cz * pull_z)
        spread = spread + jnp.where(dead, 0.0, term)
        for k, v in enumerate([mass, pull_x, pull_y, pull_z]):
            sums[k, crow, :] += jnp.where(dead, 0.0, v)
        return spread, count

    init = (jnp.zeros((WIN, 128), F32), jnp.zeros((ch, 128), F32))
    spread, count = lax.fori_loop(0, nchunk, chunk, init)
    stats[0:1, :] = jnp.sum(spread, axis=0, keepdims=True)
    stats[1:2, :] = jnp.sum(count, axis=0, keepdims=True)


def smooth_kernel(
    nblk, nnbr, nbrs, first, sums, own, win, out, stats,
    ref_a, ref_z, ref_t, table, kern, mrow, obuf,
):
    rows = own.shape[1]
    scale = LOG2E / (2.0 * KERNEL_VAR)
    root = math.sqrt(scale)
    for ref in (ref_a, ref_z, ref_t, mrow):
        ref[...] = jnp.zeros_like(ref)
    mrow[pl.ds(9, rows, stride=16), :] = jnp.ones((rows, 128), F32)

    def chunk(ck, carry):
        orow = pl.ds(pl.multiple_of(ck * H, H), H)
        wrow = pl.ds(pl.multiple_of(ck * H, H), WIN)
        origin = (first[0] + ck * H + H // 2).astype(F32)
        z0 = own[2, pl.ds(pl.multiple_of(ck * H, H), 8), :][0:1, 0:1]
        lane_features(
            ref_a, ref_z, own[0, orow, :] - origin, own[1, orow, :], own[2, orow, :] - z0,
            scale, root,
        )
        row_features(
            ref_t, win[0, wrow, :] - origin, win[1, wrow, :], win[2, wrow, :] - z0, scale, root
        )
        transpose_features(ref_t, table)

        def step(i, carry):
            for j in range(2):
                b = i * 2 + j
                at = ck * H + b
                for s in range(nnbr):
                    l = nbrs[at * nnbr + s] - (ck * H - REACH)
                    l = jnp.clip(l, 0, WIN - 1)
                    w = pair_weights(table, ref_a, ref_z, l, b)
                    kern[at, s * 128 : (s + 1) * 128, :] = w.astype(BF16)
            return carry

        lax.fori_loop(0, H // 2, step, 0)
        return carry

    lax.fori_loop(0, rows // H, chunk, 0)

    def store_motion(motion):
        for k, v in enumerate(motion):
            for t, piece in enumerate(split3(v)):
                mrow[pl.ds(3 * k + t, rows, stride=16), :] = piece

    store_motion([sums[1 + c] / (sums[0] + SHRINK) for c in range(3)])
    for r in range(1, SMOOTH + 1):
        lo = FRONT - REACH * (SMOOTH - r)
        n = nblk + 2 * REACH * (SMOOTH - r)

        def step(i, carry):
            for u in range(2):
                at = lo + i * 2 + u
                left = []
                for s in range(nnbr):
                    j = jnp.clip(nbrs[at * nnbr + s], 0, rows - 1)
                    left.append(mrow[pl.ds(pl.multiple_of(j * 16, 16), 16), :].astype(BF16))
                o = jnp.dot(
                    jnp.concatenate(left, axis=1), kern[at], preferred_element_type=F32
                )
                obuf[pl.ds(pl.multiple_of(at * 16, 16), 16), :] = o
            return carry

        if r == 1:
            obuf[...] = jnp.ones_like(obuf)
        lax.fori_loop(0, n // 2, step, 0)
        norm = obuf[pl.ds(9, rows, stride=16), :]
        motion = []
        for c in range(3):
            v = obuf[pl.ds(3 * c, rows, stride=16), :]
            v = v + obuf[pl.ds(3 * c + 1, rows, stride=16), :]
            v = v + obuf[pl.ds(3 * c + 2, rows, stride=16), :]
            motion.append(v / norm)
        if r < SMOOTH:
            store_motion(motion)
    mine = slice(FRONT, FRONT + nblk)
    mass = sums[0, mine, :]
    cross = jnp.zeros((nblk, 128), F32)
    energy = jnp.zeros((nblk, 128), F32)
    for c in range(3):
        m = motion[c][mine]
        out[c] = m
        cross = cross + sums[1 + c, mine, :] * m
        energy = energy + m * m
    stats[0:1, :] = jnp.sum(cross, axis=0, keepdims=True)
    stats[1:2, :] = jnp.sum(mass * energy, axis=0, keepdims=True)


def halo(first, last, axis):
    size = lax.axis_size(axis)
    up = [(i, i + 1) for i in range(size - 1)]
    down = [(i + 1, i) for i in range(size - 1)]
    return lax.ppermute(last, axis, up), lax.ppermute(first, axis, down)


def body(points, centroids, pair_blocks, pair_count, centroid_nbrs, sigma2):
    index_here = lax.axis_index("cells")
    nblk = centroids.shape[1] // 128
    pblk = points.shape[1] // 128
    nslot, nnbr = pair_blocks.shape[1], centroid_nbrs.shape[1]
    per_home = pblk // nblk
    ch = H * per_home
    nchunk = nblk // H
    rows = nblk + 2 * FRONT
    base = index_here * nblk
    pts = points.reshape(3, pblk, 128)
    cen = centroids.reshape(3, nblk, 128)
    before, after = halo(cen[:, :HALO], cen[:, nblk - HALO :], "cells")
    ext = jnp.concatenate([before, cen, after], axis=1)
    nbr_before, nbr_after = halo(
        centroid_nbrs[:FRONT], centroid_nbrs[nblk - FRONT :], "cells"
    )
    nbrs = jnp.concatenate([nbr_before, centroid_nbrs, nbr_after], axis=0) - (base - FRONT)
    lists = (pair_blocks - (base - REACH)).reshape(-1)
    totals = jnp.sum(pair_count.reshape(nchunk, ch), axis=1)
    start = jnp.reshape(base, (1,)).astype(jnp.int32)
    smem = pl.BlockSpec(memory_space=pltpu.SMEM)
    vmem = pl.BlockSpec(memory_space=pltpu.VMEM)
    most = ch * nslot + UNROLL
    crows = nblk + WIN - H
    features = [
        pltpu.VMEM((ch * KF, 128), F32),
        pltpu.VMEM((ch * KF, 128), F32),
        pltpu.VMEM((WIN * KF, 128), F32),
        pltpu.VMEM((WIN, 128, KF), BF16),
    ]
    params = pltpu.CompilerParams(vmem_limit_bytes=50 * 1024 * 1024)
    sums, stats = pl.pallas_call(
        functools.partial(pair_kernel, nslot, per_home, nchunk),
        out_shape=(
            jax.ShapeDtypeStruct((4, crows, 128), F32),
            jax.ShapeDtypeStruct((2, 128), F32),
        ),
        in_specs=[smem] * 5 + [vmem] * 2,
        out_specs=(vmem, vmem),
        scratch_shapes=features
        + [
            pltpu.VMEM((most, 128, 128), BF16),
            pltpu.VMEM((ch * 8, 128), F32),
            pltpu.VMEM((ch * 16, 128), F32),
            pltpu.VMEM((WIN * 16, 128), F32),
            pltpu.SMEM((most,), jnp.int32),
            pltpu.SMEM((most,), jnp.int32),
        ],
        compiler_params=params,
        name="pairs",
    )(
        lists, pair_count, totals, start, sigma2, pts,
        ext[:, HALO - REACH : HALO - REACH + crows],
    )
    sums = sums[:, : nblk + 2 * REACH]
    reach = FRONT + REACH
    from_left, from_right = halo(sums[:, :reach], sums[:, nblk + 2 * REACH - reach :], "cells")
    zeros = FRONT - REACH
    whole = jnp.pad(sums, ((0, 0), (zeros, zeros), (0, 0)))
    pad = rows - reach
    whole = whole + jnp.pad(from_left, ((0, 0), (0, pad), (0, 0)))
    whole = whole + jnp.pad(from_right, ((0, 0), (pad, 0), (0, 0)))
    off = HALO - FRONT
    motion, more = pl.pallas_call(
        functools.partial(smooth_kernel, nblk, nnbr),
        out_shape=(
            jax.ShapeDtypeStruct((3, nblk, 128), F32),
            jax.ShapeDtypeStruct((2, 128), F32),
        ),
        in_specs=[smem] * 2 + [vmem] * 3,
        out_specs=(vmem, vmem),
        scratch_shapes=[
            pltpu.VMEM((H * KF, 128), F32),
            pltpu.VMEM((H * KF, 128), F32),
            pltpu.VMEM((WIN * KF, 128), F32),
            pltpu.VMEM((WIN, 128, KF), BF16),
            pltpu.VMEM((rows, 128 * nnbr, 128), BF16),
            pltpu.VMEM((rows * 16, 128), F32),
            pltpu.VMEM((rows * 16, 128), F32),
        ],
        compiler_params=params,
        name="smoothing",
    )(
        nbrs.reshape(-1), start - FRONT, whole, ext[:, off : off + rows],
        ext[:, off - REACH : off - REACH + rows - H + WIN],
    )
    totals4 = lax.psum(jnp.concatenate([stats, more]), "cells")
    spread, count, cross, energy = [jnp.sum(totals4[i]) for i in range(4)]
    sigma_new = (spread - 2.0 * cross + energy) / (3.0 * count)
    return (motion.reshape(3, nblk * 128), jnp.reshape(sigma_new, (1,)))


def solution(mesh):
    return jax.shard_map(
        body,
        mesh=mesh,
        in_specs=(
            P(None, ("groups", "cells")),
            P(None, ("groups", "cells")),
            P(("groups", "cells"), None),
            P(("groups", "cells")),
            P(("groups", "cells"), None),
            P("groups"),
        ),
        out_specs=(P(None, ("groups", "cells")), P("groups")),
        check_vma=False,
    )
```

time: 1290 us -> 388 us (0.30)
  waiting for transfers between devices: 570 us -> 1.33 us
  other arithmetic: 283 us -> 0.93 us
  matrix products: 175 us -> 0 us
  Pallas kernels: 0 us -> 171 us
  starting transfers between devices: 36.9 us -> 170 us
  loops' own time: 89.2 us -> 0 us
  local copies, waits for them, and re-layouts: 88.1 us -> 4.21 us
    ppermute x12 -> x6, waiting for transfers between devices: 570 us -> 1.33 us  [halo(): return (lax.ppermute(last, axis, up), lax.ppermute(first, axis, down))]
    reduce_sum x50 -> x2, other arithmetic: 235 us -> 0.81 us  [the longest x1 0.69 us: body(): spread, count, cross, energy = [jnp.sum(totals4[i]) for i in range(4)]]
    dot_general x48 -> x0, matrix products: 175 us -> none  [the longest x32 171 us: group_smooth(): jnp.einsum('sjab,ksjb->ksa', kernel, nbr_motion, precision=lax.Precision....]
    pallas_call x0 -> x2, Pallas kernels: none -> 171 us  [the longest x1 96.9 us: body(): pl.pallas_call(functools.partial(pair_kernel, nslot, per_home, nchunk), o...]
    ppermute x12 -> x6, starting transfers between devices: 36.9 us -> 170 us  [halo(): return (lax.ppermute(last, axis, up), lax.ppermute(first, axis, down))]
    another operation x22 -> x0, loops' own time: 89.2 us -> none  [the longest x8 27.5 us: group_step(): lax.fori_loop(0, slot_limit, second_pass, (jnp.zeros((4, window_blocks, 1...]
    gather x72 -> x0, local copies, waits for them, and re-layouts: 46.2 us -> none  [the longest x32 21 us: slot_tile(): cen_tile = jnp.take(ext_blocks, slot_local, axis=1)]
    dynamic_slice x56 -> x0, local copies, waits for them, and re-layouts: 29 us -> none  [the longest x48 28.9 us: body(): lax.scan(group_step, init, jnp.arange(ngroup))]
  transfers between devices with their start and end apart: 12 -> 6, of which waited for: 4 -> 1; matrix products, arithmetic and copies ran while one was open for 4% -> 0% of each run, Pallas kernels for 0% -> 25%
where the time goes in v1:
time: 388 us; the launch traced here: 385 us
  Pallas kernels  171 us (44%)
  starting transfers between devices  170 us (44%)
  blocking collectives  31.8 us (8%)
  between operations  5.26 us (1%)
  local copies, waits for them, and re-layouts  4.21 us (1%)
    ppermute x6, starting transfers between devices, halo(): return (lax.ppermute(last, axis, up), lax.ppermute(first, axis, down))  170 us
    pallas_call x1, Pallas kernels, body(): pl.pallas_call(functools.partial(pair_kernel, nslot, per_home, nchunk), o...  96.9 us
    pallas_call x1, Pallas kernels, body(): pl.pallas_call(functools.partial(smooth_kernel, nblk, nnbr), out_shape=(j...  74.6 us
    psum x1, blocking collectives, body(): totals4 = lax.psum(jnp.concatenate([stats, more]), 'cells')  31.8 us
  transfers between devices with their start and end apart: 6, of which 1 were waited for; matrix products, arithmetic and copies ran while one was open for 0% of the time, Pallas kernels for 25%

profile of v1, /device:TPU:0, one launch (start us, length us, event | category | flops | bytes accessed | tf_op | source)
XLA Modules:
  0.0 385.0 jit_solution(17168612774600748911)
XLA Ops:
  0.6 0.0 copy-start.4
  0.6 0.0 copy-start.1
  0.6 1.1 copy.22
  1.7 2.4 collective-permute-start.2
  4.1 1.3 collective-permute-start.3
  5.4 0.8 fusion.2
  6.2 5.2 %collective-permute-start = (s32[16,3]{0,1:T(4,128)S(1)}, s32[16,3]{0,1:T(4,128)S(1)}, u32[]{:S(2)}, u32[]{:S(2)}) collective-permute-start(s32[16,3]{0,1:T(4,128)S(1)} %get-tuple-element.18), channel_id=1, source_target_pairs={{0,1},{1,2},{2,3},{3,4},{4,5},{5,6},{6,7},{7,8},{8,9},{9,10},{10,1... | collective-permute-start | bytes 584 | tf_op jit(solution)/shard_map/ppermute | solution.py:270
  11.4 1.3 collective-permute-start.1
  12.7 0.0 copy-done.4
  12.7 0.1 copy.11
  12.9 0.2 reshape.30.lists
  13.0 0.0 copy-done.1
  13.0 0.0 copy-start
  13.1 0.0 copy-start.2
  13.1 0.1 copy.20
  13.1 0.6 copy-done
  13.7 0.1 reshape.31
  14.5 0.1 reduce_sum.45.totals
  14.6 0.0 collective-permute-done.2
  14.6 0.0 copy-done.2
  14.6 0.0 collective-permute-done.3
  14.7 96.9 %pairs.1 = (f32[4,136,128]{2,1,0:T(8,128)S(1)}, f32[2,128]{1,0:T(2,128)S(1)}) custom-call(s32[3072]{0:T(1024)S(1)} %reshape.30.lists, s32[512]{0:T(512)S(1)} %copy-done, s32[8]{0:T(128)S(1)} %reduce_sum.45.totals, s32[1]{0:T(128)} %bitcast.first, f32[1]{0:T(128)S(6)} %copy.25.sigma2, f32[3,512,128]{2,1,0:T(8,128)S(1)} %bitcast.17, f32[3,136,128]{2,1,0:T(8,128)S(1)} %slice.60.cen), custom_call_target="tpu_custom_call" | custom-call | tf_op jit(solution)/shard_map/pairs/pallas_call | solution.py:305
  111.6 0.0 copy-start.3
  111.6 158.6 %collective-permute-start.4 = (f32[4,19,128]{2,1,0:T(8,128)S(1)}, f32[4,19,128]{2,1,0:T(8,128)S(1)}, u32[]{:S(2)}, u32[]{:S(2)}) collective-permute-start(f32[4,19,128]{2,1,0:T(8,128)S(1)} %get-tuple-element.14), channel_id=1, source_target_pairs={{0,1},{1,2},{2,3},{3,4},{4,5},{5,6},{6,7},{7,8},{8,9},{9,10},{10,1... | collective-permute-start | bytes 116744 | tf_op jit(solution)/shard_map/ppermute | solution.py:270
  270.2 1.3 collective-permute-start.5
  271.5 0.0 collective-permute-done
  271.5 0.0 collective-permute-done.1
  271.5 0.0 copy-done.3
  271.6 0.1 add_subtract_fusion
  271.6 0.1 copy.10
  271.8 0.2 sub.31.nbrs
  272.0 0.0 collective-permute-done.4
  272.0 1.3 collective-permute-done.5
  273.4 74.6 %smoothing.1 = (f32[3,128,128]{2,1,0:T(8,128)S(1)}, f32[2,128]{1,0:T(2,128)S(1)}) custom-call(s32[480]{0:T(512)S(1)} %sub.31.nbrs, s32[1]{0:T(128)S(6)} %sub.32.first, f32[4,160,128]{2,1,0:T(8,128)S(1)} %pad_add_fusion.sums, f32[3,160,128]{2,1,0:T(8,128)S(1)} %slice.61.own, f32[3,168,128]{2,1,0:T(8,128)S(1)} %slice.62.win), custom_call_target="tpu_custom_call" | custom-call | tf_op jit(solution)/shard_map/smoothing/pallas_call | solution.py:337
  348.0 31.8 %psum.7 = f32[4,128]{1,0:T(4,128)S(1)} all-reduce(f32[4,128]{1,0:T(4,128)S(1)} %pad_maximum_fusion), channel_id=1, replica_groups=mesh['groups'=2,'cells'=16] {'cells'}, use_global_device_ids=true, to_apply=%region_1.2 | all-reduce | flops 512 | bytes 4096 | tf_op jit(solution)/shard_map/psum | solution.py:360
  379.8 0.7 slice_reduce_fusion
  380.4 0.8 copy.21
  (11 shorter events, 0.1 us)
Async XLA Ops:
  0.6 12.1 %copy-start.4 = (s32[512,6]{0,1:T(8,128)S(1)}, s32[512,6]{0,1:T(8,128)}, u32[]{:S(2)}) copy-start(s32[512,6]{0,1:T(8,128)} %param.8) | copy-start | bytes 36868
  0.6 12.4 %copy-start.1 = (f32[3,65536]{1,0:T(4,128)S(1)}, f32[3,65536]{1,0:T(4,128)}, u32[]{:S(2)}) copy-start(f32[3,65536]{1,0:T(4,128)} %param.6) | copy-start | bytes 2359300
  1.7 12.9 %collective-permute-start.2 = (f32[3,24,128]{2,1,0:T(8,128)S(1)}, f32[3,24,128]{2,1,0:T(8,128)S(1)}, u32[]{:S(2)}, u32[]{:S(2)}) collective-permute-start(f32[3,24,128]{2,1,0:T(8,128)S(1)} %get-tuple-element.17), channel_id=1, source_target_pairs={{0,1},{1,2},{2,3},{3,4},{4,5},{5,6},{6,7},{7,8},{8,9},{9,10},{10,1... | collective-permute-start | bytes 110600 | tf_op jit(solution)/shard_map/ppermute | solution.py:270
  4.1 10.5 %collective-permute-start.3 = (f32[3,24,128]{2,1,0:T(8,128)S(1)}, f32[3,24,128]{2,1,0:T(8,128)S(1)}, u32[]{:S(2)}, u32[]{:S(2)}) collective-permute-start(f32[3,24,128]{2,1,0:T(8,128)S(1)} %get-tuple-element.16), channel_id=1, source_target_pairs={{1,0},{2,1},{3,2},{4,3},{5,4},{6,5},{7,6},{8,7},{9,8},{10,9},{11,1... | collective-permute-start | bytes 110600 | tf_op jit(solution)/shard_map/ppermute | solution.py:270
  6.2 265.3 %collective-permute-start = (s32[16,3]{0,1:T(4,128)S(1)}, s32[16,3]{0,1:T(4,128)S(1)}, u32[]{:S(2)}, u32[]{:S(2)}) collective-permute-start(s32[16,3]{0,1:T(4,128)S(1)} %get-tuple-element.18), channel_id=1, source_target_pairs={{0,1},{1,2},{2,3},{3,4},{4,5},{5,6},{6,7},{7,8},{8,9},{9,10},{10,1... | collective-permute-start | bytes 584 | tf_op jit(solution)/shard_map/ppermute | solution.py:270
  11.4 260.2 %collective-permute-start.1 = (s32[16,3]{0,1:T(4,128)S(1)}, s32[16,3]{0,1:T(4,128)S(1)}, u32[]{:S(2)}, u32[]{:S(2)}) collective-permute-start(s32[16,3]{0,1:T(4,128)S(1)} %get-tuple-element.19), channel_id=1, source_target_pairs={{1,0},{2,1},{3,2},{4,3},{5,4},{6,5},{7,6},{8,7},{9,8},{10,9},{11,1... | collective-permute-start | bytes 584 | tf_op jit(solution)/shard_map/ppermute | solution.py:270
  13.0 0.7 copy-start
  13.1 1.5 copy-start.2
  111.6 159.9 %copy-start.3 = (s32[128,3]{0,1:T(4,128)S(1)}, s32[128,3]{0,1:T(4,128)}, u32[]{:S(2)}) copy-start(s32[128,3]{0,1:T(4,128)} %param.10) | copy-start | bytes 4612
  111.6 160.4 %collective-permute-start.4 = (f32[4,19,128]{2,1,0:T(8,128)S(1)}, f32[4,19,128]{2,1,0:T(8,128)S(1)}, u32[]{:S(2)}, u32[]{:S(2)}) collective-permute-start(f32[4,19,128]{2,1,0:T(8,128)S(1)} %get-tuple-element.14), channel_id=1, source_target_pairs={{0,1},{1,2},{2,3},{3,4},{4,5},{5,6},{6,7},{7,8},{8,9},{9,10},{10,1... | collective-permute-start | bytes 116744 | tf_op jit(solution)/shard_map/ppermute | solution.py:270
  270.2 3.1 collective-permute-start.5

commit v2 on v1

--- a/solution.py
+++ b/solution.py
@@ -20,7 +20,7 @@
 H = 16
 WIN = 24
 DUMMY = WIN - 1
-UNROLL = 4
+UNROLL = 32
 HALO = 24
 FRONT = 16
 
@@ -61,13 +61,13 @@
 
 def transpose_features(ref_t, table):
     def step(i, carry):
-        for u in range(4):
-            j = i * 4 + u
+        for u in range(8):
+            j = i * 8 + u
             block = ref_t[pl.ds(pl.multiple_of(j * KF, KF), KF), :]
             table[j] = block.T.astype(BF16)
         return carry
 
-    lax.fori_loop(0, WIN // 4, step, 0)
+    lax.fori_loop(0, WIN // 8, step, 0)
 
 
 def pair_weights(table, ref_a, ref_z, l, b):
@@ -200,8 +200,8 @@
         transpose_features(ref_t, table)
 
         def step(i, carry):
-            for j in range(2):
-                b = i * 2 + j
+            for j in range(8):
+                b = i * 8 + j
                 at = ck * H + b
                 for s in range(nnbr):
                     l = nbrs[at * nnbr + s] - (ck * H - REACH)
@@ -210,7 +210,7 @@
                     kern[at, s * 128 : (s + 1) * 128, :] = w.astype(BF16)
             return carry
 
-        lax.fori_loop(0, H // 2, step, 0)
+        lax.fori_loop(0, H // 8, step, 0)
         return carry
 
     lax.fori_loop(0, rows // H, chunk, 0)
@@ -226,8 +226,8 @@
         n = nblk + 2 * REACH * (SMOOTH - r)
 
         def step(i, carry):
-            for u in range(2):
-                at = lo + i * 2 + u
+            for u in range(8):
+                at = lo + i * 8 + u
                 left = []
                 for s in range(nnbr):
                     j = jnp.clip(nbrs[at * nnbr + s], 0, rows - 1)
@@ -240,7 +240,7 @@
 
         if r == 1:
             obuf[...] = jnp.ones_like(obuf)
-        lax.fori_loop(0, n // 2, step, 0)
+        lax.fori_loop(0, (n + 7) // 8, step, 0)
         norm = obuf[pl.ds(9, rows, stride=16), :]
         motion = []
         for c in range(3):

time: 388 us -> 220 us (0.57); the launches traced: 385 us -> 221 us
  starting transfers between devices: 170 us -> 15.6 us
  Pallas kernels: 171 us -> 91.2 us
  blocking collectives: 31.8 us -> 100 us
    ppermute x6, starting transfers between devices: 170 us -> 15.6 us  [halo(): return (lax.ppermute(last, axis, up), lax.ppermute(first, axis, down))]
    psum x1, blocking collectives: 31.8 us -> 100 us  [body(): totals4 = lax.psum(jnp.concatenate([stats, more]), 'cells')]
    pallas_call x1, Pallas kernels: 96.9 us -> 51.5 us  [body(): pl.pallas_call(functools.partial(pair_kernel, nslot, per_home, nchunk), o...]
    pallas_call x1, Pallas kernels: 74.6 us -> 39.7 us  [body(): pl.pallas_call(functools.partial(smooth_kernel, nblk, nnbr), out_shape=(j...]
  transfers between devices with their start and end apart: 6 -> 6, of which waited for: 1 -> 1; matrix products, arithmetic and copies ran while one was open for 0% -> 1% of each run, Pallas kernels for 25% -> 23%
where the time goes in v2:
time: 220 us; the launch traced here: 221 us
  blocking collectives  100 us (45%)
  Pallas kernels  91.2 us (41%)
  starting transfers between devices  15.6 us (7%)
  between operations  5.26 us (2%)
  local copies, waits for them, and re-layouts  4.21 us (2%)
  waiting for transfers between devices  4.01 us (2%)
    psum x1, blocking collectives, body(): totals4 = lax.psum(jnp.concatenate([stats, more]), 'cells')  100 us
    pallas_call x1, Pallas kernels, body(): pl.pallas_call(functools.partial(pair_kernel, nslot, per_home, nchunk), o...  51.5 us
    pallas_call x1, Pallas kernels, body(): pl.pallas_call(functools.partial(smooth_kernel, nblk, nnbr), out_shape=(j...  39.7 us
    ppermute x6, starting transfers between devices, halo(): return (lax.ppermute(last, axis, up), lax.ppermute(first, axis, down))  15.6 us
  transfers between devices with their start and end apart: 6, of which 1 were waited for; matrix products, arithmetic and copies ran while one was open for 1% of the time, Pallas kernels for 23%

profile of v2, /device:TPU:0, one launch (start us, length us, event | category | flops | bytes accessed | tf_op | source)
XLA Modules:
  0.0 221.4 jit_solution(15099852666563812978)
XLA Ops:
  0.6 0.0 copy-start.4
  0.6 0.0 copy-start.1
  0.6 1.1 copy.22
  1.7 2.4 %collective-permute-start.2 = (f32[3,24,128]{2,1,0:T(8,128)S(1)}, f32[3,24,128]{2,1,0:T(8,128)S(1)}, u32[]{:S(2)}, u32[]{:S(2)}) collective-permute-start(f32[3,24,128]{2,1,0:T(8,128)S(1)} %get-tuple-element.17), channel_id=1, source_target_pairs={{0,1},{1,2},{2,3},{3,4},{4,5},{5,6},{6,7},{7,8},{8,9},{9,10},{10,1... | collective-permute-start | bytes 110600 | tf_op jit(solution)/shard_map/ppermute | solution.py:270
  4.1 1.3 collective-permute-start.3
  5.4 0.8 fusion.2
  6.2 5.2 %collective-permute-start = (s32[16,3]{0,1:T(4,128)S(1)}, s32[16,3]{0,1:T(4,128)S(1)}, u32[]{:S(2)}, u32[]{:S(2)}) collective-permute-start(s32[16,3]{0,1:T(4,128)S(1)} %get-tuple-element.18), channel_id=1, source_target_pairs={{0,1},{1,2},{2,3},{3,4},{4,5},{5,6},{6,7},{7,8},{8,9},{9,10},{10,1... | collective-permute-start | bytes 584 | tf_op jit(solution)/shard_map/ppermute | solution.py:270
  11.4 1.3 collective-permute-start.1
  12.7 0.0 copy-done.4
  12.7 0.1 copy.11
  12.9 0.2 reshape.30.lists
  13.0 0.0 copy-done.1
  13.0 0.0 copy-start
  13.1 0.0 copy-start.2
  13.1 0.1 copy.20
  13.1 0.6 copy-done
  13.7 0.1 reshape.31
  14.5 0.1 reduce_sum.45.totals
  14.6 0.0 collective-permute-done.2
  14.6 0.0 copy-done.2
  14.6 0.0 collective-permute-done.3
  14.7 51.5 %pairs.1 = (f32[4,136,128]{2,1,0:T(8,128)S(1)}, f32[2,128]{1,0:T(2,128)S(1)}) custom-call(s32[3072]{0:T(1024)S(1)} %reshape.30.lists, s32[512]{0:T(512)S(1)} %copy-done, s32[8]{0:T(128)S(1)} %reduce_sum.45.totals, s32[1]{0:T(128)} %bitcast.first, f32[1]{0:T(128)S(6)} %copy.25.sigma2, f32[3,512,128]{2,1,0:T(8,128)S(1)} %bitcast.17, f32[3,136,128]{2,1,0:T(8,128)S(1)} %slice.60.cen), custom_call_target="tpu_custom_call" | custom-call | tf_op jit(solution)/shard_map/pairs/pallas_call | solution.py:305
  66.1 0.0 copy-start.3
  66.2 4.2 %collective-permute-start.4 = (f32[4,19,128]{2,1,0:T(8,128)S(1)}, f32[4,19,128]{2,1,0:T(8,128)S(1)}, u32[]{:S(2)}, u32[]{:S(2)}) collective-permute-start(f32[4,19,128]{2,1,0:T(8,128)S(1)} %get-tuple-element.14), channel_id=1, source_target_pairs={{0,1},{1,2},{2,3},{3,4},{4,5},{5,6},{6,7},{7,8},{8,9},{9,10},{10,1... | collective-permute-start | bytes 116744 | tf_op jit(solution)/shard_map/ppermute | solution.py:270
  70.4 1.3 collective-permute-start.5
  71.7 0.0 collective-permute-done
  71.7 0.0 collective-permute-done.1
  71.7 0.0 copy-done.3
  71.7 0.1 add_subtract_fusion
  71.8 0.1 copy.10
  71.9 0.2 sub.31.nbrs
  72.2 0.0 collective-permute-done.4
  72.2 4.0 %collective-permute-done.5 = f32[4,19,128]{2,1,0:T(8,128)S(1)} collective-permute-done((f32[4,19,128]{2,1,0:T(8,128)S(1)}, f32[4,19,128]{2,1,0:T(8,128)S(1)}, u32[]{:S(2)}, u32[]{:S(2)}) %collective-permute-start.5) | collective-permute-done | bytes 38944 | tf_op jit(solution)/shard_map/ppermute | solution.py:270
  76.3 39.7 %smoothing.1 = (f32[3,128,128]{2,1,0:T(8,128)S(1)}, f32[2,128]{1,0:T(2,128)S(1)}) custom-call(s32[480]{0:T(512)S(1)} %sub.31.nbrs, s32[1]{0:T(128)S(6)} %sub.32.first, f32[4,160,128]{2,1,0:T(8,128)S(1)} %pad_add_fusion.sums, f32[3,160,128]{2,1,0:T(8,128)S(1)} %slice.61.own, f32[3,168,128]{2,1,0:T(8,128)S(1)} %slice.62.win), custom_call_target="tpu_custom_call" | custom-call | tf_op jit(solution)/shard_map/smoothing/pallas_call | solution.py:337
  116.0 100.2 %psum.7 = f32[4,128]{1,0:T(4,128)S(1)} all-reduce(f32[4,128]{1,0:T(4,128)S(1)} %pad_maximum_fusion), channel_id=1, replica_groups=mesh['groups'=2,'cells'=16] {'cells'}, use_global_device_ids=true, to_apply=%region_1.2 | all-reduce | flops 512 | bytes 4096 | tf_op jit(solution)/shard_map/psum | solution.py:360
  216.2 0.7 slice_reduce_fusion
  216.9 0.8 copy.21
  (11 shorter events, 0.1 us)
Async XLA Ops:
  0.6 12.1 %copy-start.4 = (s32[512,6]{0,1:T(8,128)S(1)}, s32[512,6]{0,1:T(8,128)}, u32[]{:S(2)}) copy-start(s32[512,6]{0,1:T(8,128)} %param.8) | copy-start | bytes 36868
  0.6 12.4 %copy-start.1 = (f32[3,65536]{1,0:T(4,128)S(1)}, f32[3,65536]{1,0:T(4,128)}, u32[]{:S(2)}) copy-start(f32[3,65536]{1,0:T(4,128)} %param.6) | copy-start | bytes 2359300
  1.7 12.9 %collective-permute-start.2 = (f32[3,24,128]{2,1,0:T(8,128)S(1)}, f32[3,24,128]{2,1,0:T(8,128)S(1)}, u32[]{:S(2)}, u32[]{:S(2)}) collective-permute-start(f32[3,24,128]{2,1,0:T(8,128)S(1)} %get-tuple-element.17), channel_id=1, source_target_pairs={{0,1},{1,2},{2,3},{3,4},{4,5},{5,6},{6,7},{7,8},{8,9},{9,10},{10,1... | collective-permute-start | bytes 110600 | tf_op jit(solution)/shard_map/ppermute | solution.py:270
  4.1 10.5 %collective-permute-start.3 = (f32[3,24,128]{2,1,0:T(8,128)S(1)}, f32[3,24,128]{2,1,0:T(8,128)S(1)}, u32[]{:S(2)}, u32[]{:S(2)}) collective-permute-start(f32[3,24,128]{2,1,0:T(8,128)S(1)} %get-tuple-element.16), channel_id=1, source_target_pairs={{1,0},{2,1},{3,2},{4,3},{5,4},{6,5},{7,6},{8,7},{9,8},{10,9},{11,1... | collective-permute-start | bytes 110600 | tf_op jit(solution)/shard_map/ppermute | solution.py:270
  6.2 65.5 %collective-permute-start = (s32[16,3]{0,1:T(4,128)S(1)}, s32[16,3]{0,1:T(4,128)S(1)}, u32[]{:S(2)}, u32[]{:S(2)}) collective-permute-start(s32[16,3]{0,1:T(4,128)S(1)} %get-tuple-element.18), channel_id=1, source_target_pairs={{0,1},{1,2},{2,3},{3,4},{4,5},{5,6},{6,7},{7,8},{8,9},{9,10},{10,1... | collective-permute-start | bytes 584 | tf_op jit(solution)/shard_map/ppermute | solution.py:270
  11.4 60.3 %collective-permute-start.1 = (s32[16,3]{0,1:T(4,128)S(1)}, s32[16,3]{0,1:T(4,128)S(1)}, u32[]{:S(2)}, u32[]{:S(2)}) collective-permute-start(s32[16,3]{0,1:T(4,128)S(1)} %get-tuple-element.19), channel_id=1, source_target_pairs={{1,0},{2,1},{3,2},{4,3},{5,4},{6,5},{7,6},{8,7},{9,8},{10,9},{11,1... | collective-permute-start | bytes 584 | tf_op jit(solution)/shard_map/ppermute | solution.py:270
  13.0 0.7 copy-start
  13.1 1.5 copy-start.2
  66.1 5.6 %copy-start.3 = (s32[128,3]{0,1:T(4,128)S(1)}, s32[128,3]{0,1:T(4,128)}, u32[]{:S(2)}) copy-start(s32[128,3]{0,1:T(4,128)} %param.10) | copy-start | bytes 4612
  66.2 6.1 %collective-permute-start.4 = (f32[4,19,128]{2,1,0:T(8,128)S(1)}, f32[4,19,128]{2,1,0:T(8,128)S(1)}, u32[]{:S(2)}, u32[]{:S(2)}) collective-permute-start(f32[4,19,128]{2,1,0:T(8,128)S(1)} %get-tuple-element.14), channel_id=1, source_target_pairs={{0,1},{1,2},{2,3},{3,4},{4,5},{5,6},{6,7},{7,8},{8,9},{9,10},{10,1... | collective-permute-start | bytes 116744 | tf_op jit(solution)/shard_map/ppermute | solution.py:270
  70.4 5.8 %collective-permute-start.5 = (f32[4,19,128]{2,1,0:T(8,128)S(1)}, f32[4,19,128]{2,1,0:T(8,128)S(1)}, u32[]{:S(2)}, u32[]{:S(2)}) collective-permute-start(f32[4,19,128]{2,1,0:T(8,128)S(1)} %get-tuple-element.15), channel_id=1, source_target_pairs={{1,0},{2,1},{3,2},{4,3},{5,4},{6,5},{7,6},{8,7},{9,8},{10,9},{11,1... | collective-permute-start | bytes 116744 | tf_op jit(solution)/shard_map/ppermute | solution.py:270

commit v3 on v2

--- a/solution.py
+++ b/solution.py
@@ -268,6 +268,17 @@
     up = [(i, i + 1) for i in range(size - 1)]
     down = [(i + 1, i) for i in range(size - 1)]
     return lax.ppermute(last, axis, up), lax.ppermute(first, axis, down)
+
+
+def axis_total(x, axis):
+    size = lax.axis_size(axis)
+    if size & (size - 1):
+        return lax.psum(x, axis)
+    step = 1
+    while step < size:
+        x = x + lax.ppermute(x, axis, [(i, i ^ step) for i in range(size)])
+        step *= 2
+    return x
 
 
 def body(points, centroids, pair_blocks, pair_count, centroid_nbrs, sigma2):
@@ -357,7 +368,7 @@
         nbrs.reshape(-1), start - FRONT, whole, ext[:, off : off + rows],
         ext[:, off - REACH : off - REACH + rows - H + WIN],
     )
-    totals4 = lax.psum(jnp.concatenate([stats, more]), "cells")
+    totals4 = axis_total(jnp.concatenate([stats, more]), "cells")
     spread, count, cross, energy = [jnp.sum(totals4[i]) for i in range(4)]
     sigma_new = (spread - 2.0 * cross + energy) / (3.0 * count)
     return (motion.reshape(3, nblk * 128), jnp.reshape(sigma_new, (1,)))

time: 220 us -> 204 us (0.927)
  blocking collectives: 100 us -> 0 us
  Pallas kernels: 91.2 us -> 157 us
  starting transfers between devices: 15.6 us -> 26.4 us
  waiting for transfers between devices: 4.01 us -> 10.8 us
    psum x1 -> x0, blocking collectives: 100 us -> none  [body(): totals4 = lax.psum(jnp.concatenate([stats, more]), 'cells')]
    pallas_call x1, Pallas kernels: 51.5 us -> 117 us  [body(): pl.pallas_call(functools.partial(pair_kernel, nslot, per_home, nchunk), o...]
    ppermute x0 -> x4, starting transfers between devices: none -> 13.7 us  [axis_total(): x = x + lax.ppermute(x, axis, [(i, i ^ step) for i in range(size)])]
    ppermute x0 -> x4, waiting for transfers between devices: none -> 5.3 us  [axis_total(): x = x + lax.ppermute(x, axis, [(i, i ^ step) for i in range(size)])]
    ppermute x6, starting transfers between devices: 15.6 us -> 12.7 us  [halo(): return (lax.ppermute(last, axis, up), lax.ppermute(first, axis, down))]
  transfers between devices with their start and end apart: 6 -> 10, of which waited for: 1 -> 5; matrix products, arithmetic and copies ran while one was open for 1% -> 1% of each run, Pallas kernels for 23% -> 57%
where the time goes in v3:
time: 204 us; the launch traced here: 205 us
  Pallas kernels  157 us (77%)
  starting transfers between devices  26.4 us (13%)
  waiting for transfers between devices  10.8 us (5%)
  between operations  5.31 us (3%)
  local copies, waits for them, and re-layouts  4.21 us (2%)
    pallas_call x1, Pallas kernels, body(): pl.pallas_call(functools.partial(pair_kernel, nslot, per_home, nchunk), o...  117 us
    pallas_call x1, Pallas kernels, body(): pl.pallas_call(functools.partial(smooth_kernel, nblk, nnbr), out_shape=(j...  39.7 us
    ppermute x4, starting transfers between devices, axis_total(): x = x + lax.ppermute(x, axis, [(i, i ^ step) for i in range(size)])  13.7 us
    ppermute x6, starting transfers between devices, halo(): return (lax.ppermute(last, axis, up), lax.ppermute(first, axis, down))  12.7 us
    ppermute x6, waiting for transfers between devices, halo(): return (lax.ppermute(last, axis, up), lax.ppermute(first, axis, down))  5.53 us
    ppermute x4, waiting for transfers between devices, axis_total(): x = x + lax.ppermute(x, axis, [(i, i ^ step) for i in range(size)])  5.3 us
  transfers between devices with their start and end apart: 10, of which 5 were waited for; matrix products, arithmetic and copies ran while one was open for 1% of the time, Pallas kernels for 57%

profile of v3, /device:TPU:0, one launch (start us, length us, event | category | flops | bytes accessed | tf_op | source)
XLA Modules:
  0.0 204.9 jit_solution(6569620640726943046)
XLA Ops:
  0.6 0.0 copy-start.4
  0.6 0.0 copy-start.1
  0.6 1.1 copy.22
  1.7 2.4 %collective-permute-start.2 = (f32[3,24,128]{2,1,0:T(8,128)S(1)}, f32[3,24,128]{2,1,0:T(8,128)S(1)}, u32[]{:S(2)}, u32[]{:S(2)}) collective-permute-start(f32[3,24,128]{2,1,0:T(8,128)S(1)} %get-tuple-element.17), channel_id=1, source_target_pairs={{0,1},{1,2},{2,3},{3,4},{4,5},{5,6},{6,7},{7,8},{8,9},{9,10},{10,1... | collective-permute-start | bytes 110600 | tf_op jit(solution)/shard_map/ppermute | solution.py:270
  4.1 1.3 collective-permute-start.3
  5.4 0.8 fusion.3
  6.2 5.2 %collective-permute-start = (s32[16,3]{0,1:T(4,128)S(1)}, s32[16,3]{0,1:T(4,128)S(1)}, u32[]{:S(2)}, u32[]{:S(2)}) collective-permute-start(s32[16,3]{0,1:T(4,128)S(1)} %get-tuple-element.18), channel_id=1, source_target_pairs={{0,1},{1,2},{2,3},{3,4},{4,5},{5,6},{6,7},{7,8},{8,9},{9,10},{10,1... | collective-permute-start | bytes 584 | tf_op jit(solution)/shard_map/ppermute | solution.py:270
  11.4 1.3 collective-permute-start.1
  12.7 0.0 copy-done.4
  12.7 0.1 copy.11
  12.9 0.2 reshape.30.lists
  13.0 0.0 copy-done.1
  13.0 0.0 copy-start
  13.1 0.0 copy-start.2
  13.1 0.1 copy.20
  13.1 0.6 copy-done
  13.7 0.1 reshape.31
  14.5 0.1 reduce_sum.45.totals
  14.6 0.0 collective-permute-done.2
  14.6 0.0 copy-done.2
  14.6 0.0 collective-permute-done.3
  14.7 117.5 %pairs.1 = (f32[4,136,128]{2,1,0:T(8,128)S(1)}, f32[2,128]{1,0:T(2,128)S(1)}) custom-call(s32[3072]{0:T(1024)S(1)} %reshape.30.lists, s32[512]{0:T(512)S(1)} %copy-done, s32[8]{0:T(128)S(1)} %reduce_sum.45.totals, s32[1]{0:T(128)} %bitcast.first, f32[1]{0:T(128)S(6)} %copy.25.sigma2, f32[3,512,128]{2,1,0:T(8,128)S(1)} %bitcast.17, f32[3,136,128]{2,1,0:T(8,128)S(1)} %slice.60.cen), custom_call_target="tpu_custom_call" | custom-call | tf_op jit(solution)/shard_map/pairs/pallas_call | solution.py:316
  132.1 0.0 copy-start.3
  132.2 1.3 collective-permute-start.4
  133.5 1.3 collective-permute-start.5
  134.8 0.0 collective-permute-done
  134.8 0.0 collective-permute-done.1
  134.8 0.0 copy-done.3
  134.8 0.1 add_subtract_fusion
  134.9 0.1 copy.10
  135.0 0.2 sub.31.nbrs
  135.3 0.0 collective-permute-done.4
  135.3 5.5 %collective-permute-done.5 = f32[4,19,128]{2,1,0:T(8,128)S(1)} collective-permute-done((f32[4,19,128]{2,1,0:T(8,128)S(1)}, f32[4,19,128]{2,1,0:T(8,128)S(1)}, u32[]{:S(2)}, u32[]{:S(2)}) %collective-permute-start.5) | collective-permute-done | bytes 38944 | tf_op jit(solution)/shard_map/ppermute | solution.py:270
  140.8 39.7 %smoothing.1 = (f32[3,128,128]{2,1,0:T(8,128)S(1)}, f32[2,128]{1,0:T(2,128)S(1)}) custom-call(s32[480]{0:T(512)S(1)} %sub.31.nbrs, s32[1]{0:T(128)S(6)} %sub.32.first, f32[4,160,128]{2,1,0:T(8,128)S(1)} %pad_add_fusion.sums, f32[3,160,128]{2,1,0:T(8,128)S(1)} %slice.61.own, f32[3,168,128]{2,1,0:T(8,128)S(1)} %slice.62.win), custom_call_target="tpu_custom_call" | custom-call | tf_op jit(solution)/shard_map/smoothing/pallas_call | solution.py:348
  180.6 2.8 %collective-permute-start.6 = (f32[4,128]{1,0:T(4,128)S(1)}, f32[4,128]{1,0:T(4,128)S(1)}, u32[]{:S(2)}, u32[]{:S(2)}) collective-permute-start(f32[4,128]{1,0:T(4,128)S(1)} %pad_maximum_fusion), channel_id=1, source_target_pairs={{0,1},{1,0},{2,3},{3,2},{4,5},{5,4},{6,7},{7,6},{8,9},{9,8},{10,11... | collective-permute-start | bytes 6152 | tf_op jit(solution)/shard_map/ppermute | solution.py:279
  183.4 0.8 collective-permute-done.6
  184.2 3.9 %collective-permute-start.7 = (f32[4,128]{1,0:T(4,128)S(1)}, f32[4,128]{1,0:T(4,128)S(1)}, u32[]{:S(2)}, u32[]{:S(2)}) collective-permute-start(f32[4,128]{1,0:T(4,128)S(1)} %fusion), channel_id=1, source_target_pairs={{0,2},{1,3},{2,0},{3,1},{4,6},{5,7},{6,4},{7,5},{8,10},{9,11},{10,... | collective-permute-start | bytes 6152 | tf_op jit(solution)/shard_map/ppermute | solution.py:279
  188.2 1.5 collective-permute-done.7
  189.7 4.7 %collective-permute-start.8 = (f32[4,128]{1,0:T(4,128)S(1)}, f32[4,128]{1,0:T(4,128)S(1)}, u32[]{:S(2)}, u32[]{:S(2)}) collective-permute-start(f32[4,128]{1,0:T(4,128)S(1)} %add.33), channel_id=1, source_target_pairs={{0,4},{1,5},{2,6},{3,7},{4,0},{5,1},{6,2},{7,3},{8,12},{9,13},{10,... | collective-permute-start | bytes 6152 | tf_op jit(solution)/shard_map/ppermute | solution.py:279
  194.4 1.6 collective-permute-done.8
  196.0 2.3 %collective-permute-start.9 = (f32[4,128]{1,0:T(4,128)S(1)}, f32[4,128]{1,0:T(4,128)S(1)}, u32[]{:S(2)}, u32[]{:S(2)}) collective-permute-start(f32[4,128]{1,0:T(4,128)S(1)} %add.34), channel_id=1, source_target_pairs={{0,8},{1,9},{2,10},{3,11},{4,12},{5,13},{6,14},{7,15},{8,0},{9,1},... | collective-permute-start | bytes 6152 | tf_op jit(solution)/shard_map/ppermute | solution.py:279
  198.2 0.8 copy.21
  199.1 1.4 collective-permute-done.9
  200.5 0.7 slice_reduce_fusion
  (15 shorter events, 0.2 us)
Async XLA Ops:
  0.6 12.1 %copy-start.4 = (s32[512,6]{0,1:T(8,128)S(1)}, s32[512,6]{0,1:T(8,128)}, u32[]{:S(2)}) copy-start(s32[512,6]{0,1:T(8,128)} %param.8) | copy-start | bytes 36868
  0.6 12.4 %copy-start.1 = (f32[3,65536]{1,0:T(4,128)S(1)}, f32[3,65536]{1,0:T(4,128)}, u32[]{:S(2)}) copy-start(f32[3,65536]{1,0:T(4,128)} %param.6) | copy-start | bytes 2359300
  1.7 12.9 %collective-permute-start.2 = (f32[3,24,128]{2,1,0:T(8,128)S(1)}, f32[3,24,128]{2,1,0:T(8,128)S(1)}, u32[]{:S(2)}, u32[]{:S(2)}) collective-permute-start(f32[3,24,128]{2,1,0:T(8,128)S(1)} %get-tuple-element.17), channel_id=1, source_target_pairs={{0,1},{1,2},{2,3},{3,4},{4,5},{5,6},{6,7},{7,8},{8,9},{9,10},{10,1... | collective-permute-start | bytes 110600 | tf_op jit(solution)/shard_map/ppermute | solution.py:270
  4.1 10.5 %collective-permute-start.3 = (f32[3,24,128]{2,1,0:T(8,128)S(1)}, f32[3,24,128]{2,1,0:T(8,128)S(1)}, u32[]{:S(2)}, u32[]{:S(2)}) collective-permute-start(f32[3,24,128]{2,1,0:T(8,128)S(1)} %get-tuple-element.16), channel_id=1, source_target_pairs={{1,0},{2,1},{3,2},{4,3},{5,4},{6,5},{7,6},{8,7},{9,8},{10,9},{11,1... | collective-permute-start | bytes 110600 | tf_op jit(solution)/shard_map/ppermute | solution.py:270
  6.2 128.5 %collective-permute-start = (s32[16,3]{0,1:T(4,128)S(1)}, s32[16,3]{0,1:T(4,128)S(1)}, u32[]{:S(2)}, u32[]{:S(2)}) collective-permute-start(s32[16,3]{0,1:T(4,128)S(1)} %get-tuple-element.18), channel_id=1, source_target_pairs={{0,1},{1,2},{2,3},{3,4},{4,5},{5,6},{6,7},{7,8},{8,9},{9,10},{10,1... | collective-permute-start | bytes 584 | tf_op jit(solution)/shard_map/ppermute | solution.py:270
  11.4 123.4 %collective-permute-start.1 = (s32[16,3]{0,1:T(4,128)S(1)}, s32[16,3]{0,1:T(4,128)S(1)}, u32[]{:S(2)}, u32[]{:S(2)}) collective-permute-start(s32[16,3]{0,1:T(4,128)S(1)} %get-tuple-element.19), channel_id=1, source_target_pairs={{1,0},{2,1},{3,2},{4,3},{5,4},{6,5},{7,6},{8,7},{9,8},{10,9},{11,1... | collective-permute-start | bytes 584 | tf_op jit(solution)/shard_map/ppermute | solution.py:270
  13.0 0.7 copy-start
  13.1 1.5 copy-start.2
  132.1 2.6 %copy-start.3 = (s32[128,3]{0,1:T(4,128)S(1)}, s32[128,3]{0,1:T(4,128)}, u32[]{:S(2)}) copy-start(s32[128,3]{0,1:T(4,128)} %param.10) | copy-start | bytes 4612
  132.2 3.1 %collective-permute-start.4 = (f32[4,19,128]{2,1,0:T(8,128)S(1)}, f32[4,19,128]{2,1,0:T(8,128)S(1)}, u32[]{:S(2)}, u32[]{:S(2)}) collective-permute-start(f32[4,19,128]{2,1,0:T(8,128)S(1)} %get-tuple-element.14), channel_id=1, source_target_pairs={{0,1},{1,2},{2,3},{3,4},{4,5},{5,6},{6,7},{7,8},{8,9},{9,10},{10,1... | collective-permute-start | bytes 116744 | tf_op jit(solution)/shard_map/ppermute | solution.py:270
  133.5 7.3 %collective-permute-start.5 = (f32[4,19,128]{2,1,0:T(8,128)S(1)}, f32[4,19,128]{2,1,0:T(8,128)S(1)}, u32[]{:S(2)}, u32[]{:S(2)}) collective-permute-start(f32[4,19,128]{2,1,0:T(8,128)S(1)} %get-tuple-element.15), channel_id=1, source_target_pairs={{1,0},{2,1},{3,2},{4,3},{5,4},{6,5},{7,6},{8,7},{9,8},{10,9},{11,1... | collective-permute-start | bytes 116744 | tf_op jit(solution)/shard_map/ppermute | solution.py:270
  180.6 3.7 %collective-permute-start.6 = (f32[4,128]{1,0:T(4,128)S(1)}, f32[4,128]{1,0:T(4,128)S(1)}, u32[]{:S(2)}, u32[]{:S(2)}) collective-permute-start(f32[4,128]{1,0:T(4,128)S(1)} %pad_maximum_fusion), channel_id=1, source_target_pairs={{0,1},{1,0},{2,3},{3,2},{4,5},{5,4},{6,7},{7,6},{8,9},{9,8},{10,11... | collective-permute-start | bytes 6152 | tf_op jit(solution)/shard_map/ppermute | solution.py:279
  184.2 5.5 %collective-permute-start.7 = (f32[4,128]{1,0:T(4,128)S(1)}, f32[4,128]{1,0:T(4,128)S(1)}, u32[]{:S(2)}, u32[]{:S(2)}) collective-permute-start(f32[4,128]{1,0:T(4,128)S(1)} %fusion), channel_id=1, source_target_pairs={{0,2},{1,3},{2,0},{3,1},{4,6},{5,7},{6,4},{7,5},{8,10},{9,11},{10,... | collective-permute-start | bytes 6152 | tf_op jit(solution)/shard_map/ppermute | solution.py:279
  189.7 6.2 %collective-permute-start.8 = (f32[4,128]{1,0:T(4,128)S(1)}, f32[4,128]{1,0:T(4,128)S(1)}, u32[]{:S(2)}, u32[]{:S(2)}) collective-permute-start(f32[4,128]{1,0:T(4,128)S(1)} %add.33), channel_id=1, source_target_pairs={{0,4},{1,5},{2,6},{3,7},{4,0},{5,1},{6,2},{7,3},{8,12},{9,13},{10,... | collective-permute-start | bytes 6152 | tf_op jit(solution)/shard_map/ppermute | solution.py:279
  196.0 4.5 %collective-permute-start.9 = (f32[4,128]{1,0:T(4,128)S(1)}, f32[4,128]{1,0:T(4,128)S(1)}, u32[]{:S(2)}, u32[]{:S(2)}) collective-permute-start(f32[4,128]{1,0:T(4,128)S(1)} %add.34), channel_id=1, source_target_pairs={{0,8},{1,9},{2,10},{3,11},{4,12},{5,13},{6,14},{7,15},{8,0},{9,1},... | collective-permute-start | bytes 6152 | tf_op jit(solution)/shard_map/ppermute | solution.py:279

commit v4 on v3

--- a/solution.py
+++ b/solution.py
@@ -20,7 +20,7 @@
 H = 16
 WIN = 24
 DUMMY = WIN - 1
-UNROLL = 32
+UNROLL = 64
 HALO = 24
 FRONT = 16
 
@@ -200,8 +200,8 @@
         transpose_features(ref_t, table)
 
         def step(i, carry):
-            for j in range(8):
-                b = i * 8 + j
+            for j in range(H):
+                b = i * H + j
                 at = ck * H + b
                 for s in range(nnbr):
                     l = nbrs[at * nnbr + s] - (ck * H - REACH)
@@ -210,7 +210,7 @@
                     kern[at, s * 128 : (s + 1) * 128, :] = w.astype(BF16)
             return carry
 
-        lax.fori_loop(0, H // 8, step, 0)
+        step(0, 0)
         return carry
 
     lax.fori_loop(0, rows // H, chunk, 0)

time: 204 us -> 197 us (0.966)
  Pallas kernels: 157 us -> 92 us
  waiting for transfers between devices: 10.8 us -> 68.8 us
    pallas_call x1, Pallas kernels: 117 us -> 54 us  [body(): pl.pallas_call(functools.partial(pair_kernel, nslot, per_home, nchunk), o...]
    ppermute x6, waiting for transfers between devices: 5.53 us -> 61.9 us  [halo(): return (lax.ppermute(last, axis, up), lax.ppermute(first, axis, down))]
    ppermute x4, starting transfers between devices: 13.7 us -> 9.31 us  [axis_total(): x = x + lax.ppermute(x, axis, [(i, i ^ step) for i in range(size)])]
    ppermute x6, starting transfers between devices: 12.7 us -> 15.7 us  [halo(): return (lax.ppermute(last, axis, up), lax.ppermute(first, axis, down))]
  transfers between devices with their start and end apart: 10 -> 10, of which waited for: 5 -> 5; matrix products, arithmetic and copies ran while one was open for 1% -> 1% of each run, Pallas kernels for 57% -> 28%
where the time goes in v4:
time: 197 us; the launch traced here: 196 us
  Pallas kernels  92 us (47%)
  waiting for transfers between devices  68.8 us (35%)
  starting transfers between devices  25 us (13%)
  between operations  5.31 us (3%)
  local copies, waits for them, and re-layouts  4.21 us (2%)
    ppermute x6, waiting for transfers between devices, halo(): return (lax.ppermute(last, axis, up), lax.ppermute(first, axis, down))  61.9 us
    pallas_call x1, Pallas kernels, body(): pl.pallas_call(functools.partial(pair_kernel, nslot, per_home, nchunk), o...  54 us
    pallas_call x1, Pallas kernels, body(): pl.pallas_call(functools.partial(smooth_kernel, nblk, nnbr), out_shape=(j...  38 us
    ppermute x6, starting transfers between devices, halo(): return (lax.ppermute(last, axis, up), lax.ppermute(first, axis, down))  15.7 us
    ppermute x4, starting transfers between devices, axis_total(): x = x + lax.ppermute(x, axis, [(i, i ^ step) for i in range(size)])  9.31 us
    ppermute x4, waiting for transfers between devices, axis_total(): x = x + lax.ppermute(x, axis, [(i, i ^ step) for i in range(size)])  6.98 us
  transfers between devices with their start and end apart: 10, of which 5 were waited for; matrix products, arithmetic and copies ran while one was open for 1% of the time, Pallas kernels for 28%

profile of v4, /device:TPU:0, one launch (start us, length us, event | category | flops | bytes accessed | tf_op | source)
XLA Modules:
  0.0 196.3 jit_solution(7354477086622721651)
XLA Ops:
  0.6 0.0 copy-start.4
  0.6 0.0 copy-start.1
  0.6 1.1 copy.22
  1.7 2.4 %collective-permute-start.2 = (f32[3,24,128]{2,1,0:T(8,128)S(1)}, f32[3,24,128]{2,1,0:T(8,128)S(1)}, u32[]{:S(2)}, u32[]{:S(2)}) collective-permute-start(f32[3,24,128]{2,1,0:T(8,128)S(1)} %get-tuple-element.17), channel_id=1, source_target_pairs={{0,1},{1,2},{2,3},{3,4},{4,5},{5,6},{6,7},{7,8},{8,9},{9,10},{10,1... | collective-permute-start | bytes 110600 | tf_op jit(solution)/shard_map/ppermute | solution.py:270
  4.1 1.3 collective-permute-start.3
  5.4 0.8 fusion.3
  6.2 5.2 %collective-permute-start = (s32[16,3]{0,1:T(4,128)S(1)}, s32[16,3]{0,1:T(4,128)S(1)}, u32[]{:S(2)}, u32[]{:S(2)}) collective-permute-start(s32[16,3]{0,1:T(4,128)S(1)} %get-tuple-element.18), channel_id=1, source_target_pairs={{0,1},{1,2},{2,3},{3,4},{4,5},{5,6},{6,7},{7,8},{8,9},{9,10},{10,1... | collective-permute-start | bytes 584 | tf_op jit(solution)/shard_map/ppermute | solution.py:270
  11.4 1.3 collective-permute-start.1
  12.7 0.0 copy-done.4
  12.7 0.1 copy.11
  12.9 0.2 reshape.30.lists
  13.0 0.0 copy-done.1
  13.0 0.0 copy-start
  13.1 0.0 copy-start.2
  13.1 0.1 copy.20
  13.1 0.6 copy-done
  13.7 0.1 reshape.31
  14.5 0.1 reduce_sum.45.totals
  14.6 0.0 collective-permute-done.2
  14.6 0.0 copy-done.2
  14.6 0.0 collective-permute-done.3
  14.7 54.0 %pairs.1 = (f32[4,136,128]{2,1,0:T(8,128)S(1)}, f32[2,128]{1,0:T(2,128)S(1)}) custom-call(s32[3072]{0:T(1024)S(1)} %reshape.30.lists, s32[512]{0:T(512)S(1)} %copy-done, s32[8]{0:T(128)S(1)} %reduce_sum.45.totals, s32[1]{0:T(128)} %bitcast.first, f32[1]{0:T(128)S(6)} %copy.25.sigma2, f32[3,512,128]{2,1,0:T(8,128)S(1)} %bitcast.17, f32[3,136,128]{2,1,0:T(8,128)S(1)} %slice.60.cen), custom_call_target="tpu_custom_call" | custom-call | tf_op jit(solution)/shard_map/pairs/pallas_call | solution.py:316
  68.7 0.0 copy-start.3
  68.7 4.3 %collective-permute-start.4 = (f32[4,19,128]{2,1,0:T(8,128)S(1)}, f32[4,19,128]{2,1,0:T(8,128)S(1)}, u32[]{:S(2)}, u32[]{:S(2)}) collective-permute-start(f32[4,19,128]{2,1,0:T(8,128)S(1)} %get-tuple-element.14), channel_id=1, source_target_pairs={{0,1},{1,2},{2,3},{3,4},{4,5},{5,6},{6,7},{7,8},{8,9},{9,10},{10,1... | collective-permute-start | bytes 116744 | tf_op jit(solution)/shard_map/ppermute | solution.py:270
  73.0 1.3 collective-permute-start.5
  74.3 0.0 collective-permute-done
  74.3 0.0 collective-permute-done.1
  74.3 0.0 copy-done.3
  74.3 0.1 add_subtract_fusion
  74.4 0.1 copy.10
  74.5 0.2 sub.31.nbrs
  74.8 0.0 collective-permute-done.4
  74.8 61.9 %collective-permute-done.5 = f32[4,19,128]{2,1,0:T(8,128)S(1)} collective-permute-done((f32[4,19,128]{2,1,0:T(8,128)S(1)}, f32[4,19,128]{2,1,0:T(8,128)S(1)}, u32[]{:S(2)}, u32[]{:S(2)}) %collective-permute-start.5) | collective-permute-done | bytes 38944 | tf_op jit(solution)/shard_map/ppermute | solution.py:270
  136.7 38.0 %smoothing.1 = (f32[3,128,128]{2,1,0:T(8,128)S(1)}, f32[2,128]{1,0:T(2,128)S(1)}) custom-call(s32[480]{0:T(512)S(1)} %sub.31.nbrs, s32[1]{0:T(128)S(6)} %sub.32.first, f32[4,160,128]{2,1,0:T(8,128)S(1)} %pad_add_fusion.sums, f32[3,160,128]{2,1,0:T(8,128)S(1)} %slice.61.own, f32[3,168,128]{2,1,0:T(8,128)S(1)} %slice.62.win), custom_call_target="tpu_custom_call" | custom-call | tf_op jit(solution)/shard_map/smoothing/pallas_call | solution.py:348
  174.7 2.9 %collective-permute-start.6 = (f32[4,128]{1,0:T(4,128)S(1)}, f32[4,128]{1,0:T(4,128)S(1)}, u32[]{:S(2)}, u32[]{:S(2)}) collective-permute-start(f32[4,128]{1,0:T(4,128)S(1)} %pad_maximum_fusion), channel_id=1, source_target_pairs={{0,1},{1,0},{2,3},{3,2},{4,5},{5,4},{6,7},{7,6},{8,9},{9,8},{10,11... | collective-permute-start | bytes 6152 | tf_op jit(solution)/shard_map/ppermute | solution.py:279
  177.5 0.8 collective-permute-done.6
  178.4 0.3 collective-permute-start.7
  178.7 3.4 %collective-permute-done.7 = f32[4,128]{1,0:T(4,128)S(1)} collective-permute-done((f32[4,128]{1,0:T(4,128)S(1)}, f32[4,128]{1,0:T(4,128)S(1)}, u32[]{:S(2)}, u32[]{:S(2)}) %collective-permute-start.7) | collective-permute-done | bytes 2080 | tf_op jit(solution)/shard_map/ppermute | solution.py:279
  182.0 1.5 collective-permute-start.8
  183.5 2.1 %collective-permute-done.8 = f32[4,128]{1,0:T(4,128)S(1)} collective-permute-done((f32[4,128]{1,0:T(4,128)S(1)}, f32[4,128]{1,0:T(4,128)S(1)}, u32[]{:S(2)}, u32[]{:S(2)}) %collective-permute-start.8) | collective-permute-done | bytes 2080 | tf_op jit(solution)/shard_map/ppermute | solution.py:279
  185.6 4.7 %collective-permute-start.9 = (f32[4,128]{1,0:T(4,128)S(1)}, f32[4,128]{1,0:T(4,128)S(1)}, u32[]{:S(2)}, u32[]{:S(2)}) collective-permute-start(f32[4,128]{1,0:T(4,128)S(1)} %add.34), channel_id=1, source_target_pairs={{0,8},{1,9},{2,10},{3,11},{4,12},{5,13},{6,14},{7,15},{8,0},{9,1},... | collective-permute-start | bytes 6152 | tf_op jit(solution)/shard_map/ppermute | solution.py:279
  190.3 0.8 copy.21
  191.1 0.7 collective-permute-done.9
  191.8 0.7 slice_reduce_fusion
  (15 shorter events, 0.2 us)
Async XLA Ops:
  0.6 12.1 %copy-start.4 = (s32[512,6]{0,1:T(8,128)S(1)}, s32[512,6]{0,1:T(8,128)}, u32[]{:S(2)}) copy-start(s32[512,6]{0,1:T(8,128)} %param.8) | copy-start | bytes 36868
  0.6 12.4 %copy-start.1 = (f32[3,65536]{1,0:T(4,128)S(1)}, f32[3,65536]{1,0:T(4,128)}, u32[]{:S(2)}) copy-start(f32[3,65536]{1,0:T(4,128)} %param.6) | copy-start | bytes 2359300
  1.7 12.9 %collective-permute-start.2 = (f32[3,24,128]{2,1,0:T(8,128)S(1)}, f32[3,24,128]{2,1,0:T(8,128)S(1)}, u32[]{:S(2)}, u32[]{:S(2)}) collective-permute-start(f32[3,24,128]{2,1,0:T(8,128)S(1)} %get-tuple-element.17), channel_id=1, source_target_pairs={{0,1},{1,2},{2,3},{3,4},{4,5},{5,6},{6,7},{7,8},{8,9},{9,10},{10,1... | collective-permute-start | bytes 110600 | tf_op jit(solution)/shard_map/ppermute | solution.py:270
  4.1 10.5 %collective-permute-start.3 = (f32[3,24,128]{2,1,0:T(8,128)S(1)}, f32[3,24,128]{2,1,0:T(8,128)S(1)}, u32[]{:S(2)}, u32[]{:S(2)}) collective-permute-start(f32[3,24,128]{2,1,0:T(8,128)S(1)} %get-tuple-element.16), channel_id=1, source_target_pairs={{1,0},{2,1},{3,2},{4,3},{5,4},{6,5},{7,6},{8,7},{9,8},{10,9},{11,1... | collective-permute-start | bytes 110600 | tf_op jit(solution)/shard_map/ppermute | solution.py:270
  6.2 68.1 %collective-permute-start = (s32[16,3]{0,1:T(4,128)S(1)}, s32[16,3]{0,1:T(4,128)S(1)}, u32[]{:S(2)}, u32[]{:S(2)}) collective-permute-start(s32[16,3]{0,1:T(4,128)S(1)} %get-tuple-element.18), channel_id=1, source_target_pairs={{0,1},{1,2},{2,3},{3,4},{4,5},{5,6},{6,7},{7,8},{8,9},{9,10},{10,1... | collective-permute-start | bytes 584 | tf_op jit(solution)/shard_map/ppermute | solution.py:270
  11.4 62.9 %collective-permute-start.1 = (s32[16,3]{0,1:T(4,128)S(1)}, s32[16,3]{0,1:T(4,128)S(1)}, u32[]{:S(2)}, u32[]{:S(2)}) collective-permute-start(s32[16,3]{0,1:T(4,128)S(1)} %get-tuple-element.19), channel_id=1, source_target_pairs={{1,0},{2,1},{3,2},{4,3},{5,4},{6,5},{7,6},{8,7},{9,8},{10,9},{11,1... | collective-permute-start | bytes 584 | tf_op jit(solution)/shard_map/ppermute | solution.py:270
  13.0 0.7 copy-start
  13.1 1.5 copy-start.2
  68.7 5.6 %copy-start.3 = (s32[128,3]{0,1:T(4,128)S(1)}, s32[128,3]{0,1:T(4,128)}, u32[]{:S(2)}) copy-start(s32[128,3]{0,1:T(4,128)} %param.10) | copy-start | bytes 4612
  68.7 6.1 %collective-permute-start.4 = (f32[4,19,128]{2,1,0:T(8,128)S(1)}, f32[4,19,128]{2,1,0:T(8,128)S(1)}, u32[]{:S(2)}, u32[]{:S(2)}) collective-permute-start(f32[4,19,128]{2,1,0:T(8,128)S(1)} %get-tuple-element.14), channel_id=1, source_target_pairs={{0,1},{1,2},{2,3},{3,4},{4,5},{5,6},{6,7},{7,8},{8,9},{9,10},{10,1... | collective-permute-start | bytes 116744 | tf_op jit(solution)/shard_map/ppermute | solution.py:270
  73.0 63.7 %collective-permute-start.5 = (f32[4,19,128]{2,1,0:T(8,128)S(1)}, f32[4,19,128]{2,1,0:T(8,128)S(1)}, u32[]{:S(2)}, u32[]{:S(2)}) collective-permute-start(f32[4,19,128]{2,1,0:T(8,128)S(1)} %get-tuple-element.15), channel_id=1, source_target_pairs={{1,0},{2,1},{3,2},{4,3},{5,4},{6,5},{7,6},{8,7},{9,8},{10,9},{11,1... | collective-permute-start | bytes 116744 | tf_op jit(solution)/shard_map/ppermute | solution.py:270
  174.7 3.7 %collective-permute-start.6 = (f32[4,128]{1,0:T(4,128)S(1)}, f32[4,128]{1,0:T(4,128)S(1)}, u32[]{:S(2)}, u32[]{:S(2)}) collective-permute-start(f32[4,128]{1,0:T(4,128)S(1)} %pad_maximum_fusion), channel_id=1, source_target_pairs={{0,1},{1,0},{2,3},{3,2},{4,5},{5,4},{6,7},{7,6},{8,9},{9,8},{10,11... | collective-permute-start | bytes 6152 | tf_op jit(solution)/shard_map/ppermute | solution.py:279
  178.4 3.6 %collective-permute-start.7 = (f32[4,128]{1,0:T(4,128)S(1)}, f32[4,128]{1,0:T(4,128)S(1)}, u32[]{:S(2)}, u32[]{:S(2)}) collective-permute-start(f32[4,128]{1,0:T(4,128)S(1)} %fusion), channel_id=1, source_target_pairs={{0,2},{1,3},{2,0},{3,1},{4,6},{5,7},{6,4},{7,5},{8,10},{9,11},{10,... | collective-permute-start | bytes 6152 | tf_op jit(solution)/shard_map/ppermute | solution.py:279
  182.0 3.6 %collective-permute-start.8 = (f32[4,128]{1,0:T(4,128)S(1)}, f32[4,128]{1,0:T(4,128)S(1)}, u32[]{:S(2)}, u32[]{:S(2)}) collective-permute-start(f32[4,128]{1,0:T(4,128)S(1)} %add.33), channel_id=1, source_target_pairs={{0,4},{1,5},{2,6},{3,7},{4,0},{5,1},{6,2},{7,3},{8,12},{9,13},{10,... | collective-permute-start | bytes 6152 | tf_op jit(solution)/shard_map/ppermute | solution.py:279
  185.6 6.2 %collective-permute-start.9 = (f32[4,128]{1,0:T(4,128)S(1)}, f32[4,128]{1,0:T(4,128)S(1)}, u32[]{:S(2)}, u32[]{:S(2)}) collective-permute-start(f32[4,128]{1,0:T(4,128)S(1)} %add.34), channel_id=1, source_target_pairs={{0,8},{1,9},{2,10},{3,11},{4,12},{5,13},{6,14},{7,15},{8,0},{9,1},... | collective-permute-start | bytes 6152 | tf_op jit(solution)/shard_map/ppermute | solution.py:279
